TPU v7x, 256 devices: a whole 4x4x8 slice. The times are simulated.
256 devices in a mesh: dp: 64 (over x, y_hi, z), tp: 4 (over y_lo, core).
Axes of the slice: x: 4, y: 4 (y_hi: 2, y_lo: 2; y = y_hi * 2 + y_lo), z: 8, core: 2. Of those that a mesh axis runs over, the one named last changes fastest.
Arguments:
- partials: bfloat16 [64, 7168, 1024], P('dp', None, 'tp'), may hold values from -4 to 4, as said below
- momentum: float32 [7168, 1024], P('dp', 'tp'), may hold values from -6 to 6
- weights: float32 [7168, 1024], P('dp', 'tp'), may hold values from -6 to 6
Outputs:
- update: float32 [7168, 1024], P('dp', 'tp')
- new_weights: float32 [7168, 1024], P('dp', 'tp')
- new_momentum: float32 [7168, 1024], P('dp', 'tp')
Inputs may be any that keep to these rules, and one draw needn't show every extreme that they name: `partials`: real-valued partial gradients.
All inputs are finite; a program needn't handle non-finite values.
Results may differ from a plain program's by a relative error of at most 0.0003.
Values sent between devices are 32-bit elements; how exact they have to be, the bound alone decides.
A program may use at most 64 MiB of HBM per device.

v0:
```python
import math

import jax
import jax.numpy as jnp
from jax import lax
from jax.sharding import PartitionSpec as P

D = 7168
FF = 1024
ITERS = 2


COEF_A = 3.4445
COEF_B = -4.775
COEF_C = 2.0315
MOMENTUM_DECAY = 0.95
LEARN_RATE = 0.02
WEIGHT_DECAY = 0.1
NORM_EPS = 1e-07


def gram_local(block):
    return lax.dot_general(
        block,
        block,
        (((0,), (0,)), ((), ())),
        precision=lax.Precision.HIGHEST,
        preferred_element_type=jnp.float32,
    )


def matmul_high(left, right):
    return jnp.dot(left, right, precision=lax.Precision.HIGHEST, preferred_element_type=jnp.float32)


def on_device(partials, momentum, weights):
    partial_terms = partials[0].astype(jnp.float32)
    gradient = lax.psum_scatter(partial_terms, "dp", scatter_dimension=0, tiled=True)
    new_momentum = MOMENTUM_DECAY * momentum + gradient
    nesterov = gradient + MOMENTUM_DECAY * new_momentum
    col_width = nesterov.shape[1]
    row_block = lax.all_gather(nesterov, "tp", axis=1, tiled=True)

    def gram_total(partial_value):
        return lax.psum(partial_value, "dp")

    first_gram = gram_total(gram_local(row_block))
    inverse_norm = 1.0 / (jnp.sqrt(jnp.trace(first_gram)) + NORM_EPS)
    current = row_block * inverse_norm
    square = first_gram * (inverse_norm * inverse_norm)
    for iteration in range(ITERS):
        if iteration > 0:
            square = gram_total(gram_local(current))
        mixing = COEF_B * square + COEF_C * matmul_high(square, square)
        current = COEF_A * current + matmul_high(current, mixing)
    result_rows = lax.dynamic_slice_in_dim(current, lax.axis_index("tp") * col_width, col_width, 1)
    update = 0.2 * math.sqrt(max(D, FF)) * result_rows
    new_weights = weights - LEARN_RATE * (update + WEIGHT_DECAY * weights)
    return (update, new_weights, new_momentum)


def solution(mesh):
    return jax.shard_map(
        on_device,
        mesh=mesh,
        in_specs=(P("dp", None, "tp"), P("dp", "tp"), P("dp", "tp")),
        out_specs=(P("dp", "tp"), P("dp", "tp"), P("dp", "tp")),
        check_vma=False,
    )
```

profile of v0, /device:TPU:8, one launch (start us, length us, event | category | flops | bytes accessed | tf_op | source)
XLA Modules:
  0.0 1864.0 jit_solution(6920116099027002787)
XLA Ops:
  7.2 0.0 reduce-scatter.2.cloned.1.call-start
  7.2 5.6 bitcast_convert_fusion
  12.8 0.0 copy-start.2
  12.8 0.0 reduce-scatter.2.cloned.1.call-update
  12.8 0.0 all-reduce.3.cloned.1.call-start
  12.9 379.5 %reduce-scatter.2.cloned.1.call-done = f32[112,256]{1,0:T(8,128)} async-done(((f32[7168,256]{1,0:T(8,128)}), f32[112,256]{1,0:T(8,128)}) %reduce-scatter.2.cloned.1.call-update) | async-done | bytes 114704 | tf_op jit(solution)/shard_map/reduce_scatter | solution.py:38
  392.4 0.0 copy-done.2
  392.4 1.6 multiply_add_fusion
  393.9 6.4 all_gather.3
  400.3 5.1 fusion.28
  405.4 0.0 all-reduce.3.cloned.1.call-update
  405.4 0.2 all-reduce.5.cloned.1.call-start
  405.7 698.8 %all-reduce.3.cloned.1.call-done = f32[1024,1024]{1,0:T(8,128)} async-done(((f32[1024,1024]{1,0:T(8,128)}), f32[1024,1024]{1,0:T(8,128)}) %all-reduce.3.cloned.1.call-update) | async-done | bytes 4194320 | tf_op jit(solution)/shard_map/psum | solution.py:45
  1104.5 2.9 select_reduce_fusion
  1108.1 0.0 copy-start
  1108.1 17.2 fusion.8
  1125.3 0.0 copy-done
  1125.3 2.9 fusion.17
  1128.2 5.1 fusion.29
  1133.3 0.0 all-reduce.5.cloned.1.call-update
  1133.4 703.2 %all-reduce.5.cloned.1.call-done = f32[1024,1024]{1,0:T(8,128)} async-done(((f32[1024,1024]{1,0:T(8,128)}), f32[1024,1024]{1,0:T(8,128)}) %all-reduce.5.cloned.1.call-update) | async-done | bytes 4194320 | tf_op jit(solution)/shard_map/psum | solution.py:45
  1836.6 0.0 copy-start.1
  1836.6 17.3 fusion.30
  1853.9 0.0 copy-done.1
  1853.9 0.0 copy-start.3
  1853.9 2.8 fusion
  1856.7 0.0 copy-done.3
  1856.7 0.7 multiply_subtract_fusion
Async XLA Ops:
  7.2 385.2 %reduce-scatter.2.cloned.1.call-start = ((), (), s32[]{:S(2)}) async-start(), calls=%async_computation.1 | async-start | bytes 7454720 | tf_op jit(solution)/shard_map/reduce_scatter | solution.py:38
  12.8 379.6 %copy-start.2 = (f32[112,256]{1,0:T(8,128)S(1)}, f32[112,256]{1,0:T(8,128)}, u32[]{:S(2)}) copy-start(f32[112,256]{1,0:T(8,128)} %param.4) | copy-start | bytes 344068
  12.8 1091.7 %all-reduce.3.cloned.1.call-start = ((), (), s32[]{:S(2)}) async-start(), calls=%async_computation.2 | async-start | bytes 8388608 | tf_op jit(solution)/shard_map/psum | solution.py:45
  405.4 1431.1 %all-reduce.5.cloned.1.call-start = ((), (), s32[]{:S(2)}) async-start(), calls=%async_computation.3 | async-start | bytes 8388608 | tf_op jit(solution)/shard_map/psum | solution.py:45
  1108.1 17.2 copy-start
  1836.6 17.3 copy-start.1
  1853.9 2.8 copy-start.3
Sparse Core Ops, SparseCore 0:
  12.9 379.4 reduce-scatter.1
  405.5 698.8 all-reduce.2
  1133.5 703.0 all-reduce.4
where the time goes:
time: 1860 us
  waiting for transfers between devices  1780 us (96%)
  matrix products  50.3 us (3%)
    psum x2, waiting for transfers between devices, gram_total(): return lax.psum(partial_value, 'dp')  1400 us
    reduce_scatter x1, waiting for transfers between devices, on_device(): lax.psum_scatter(partial_terms, 'dp', scatter_dimension=0, tiled=True)  380 us
    dot_general x4, matrix products, matmul_high(): jnp.dot(left, right, precision=lax.Precision.HIGHEST, preferred_element_t...  40.2 us
  transfers between devices with their start and end apart: 3, of which 3 were waited for; matrix products, arithmetic and copies ran while one was open for 0% of the time, Pallas kernels for 0%

commit v1 on v0

v1 whole, which is shorter than its diff:
```python
import math

import jax
import jax.numpy as jnp
from jax import lax
from jax.sharding import PartitionSpec as P

D = 7168
FF = 1024

COEF_A = 3.4445
COEF_B = -4.775
COEF_C = 2.0315
MOMENTUM_DECAY = 0.95
LEARN_RATE = 0.02
WEIGHT_DECAY = 0.1
NORM_EPS = 1e-07


def mm(left, right):
    return jnp.dot(left, right, precision=lax.Precision.HIGH, preferred_element_type=jnp.float32)


def on_device(partials, momentum, weights):
    gradient = lax.psum_scatter(partials[0].astype(jnp.float32), "dp", scatter_dimension=0, tiled=True)
    new_momentum = MOMENTUM_DECAY * momentum + gradient
    nesterov = gradient + MOMENTUM_DECAY * new_momentum
    width = nesterov.shape[1]
    rows = lax.all_gather(nesterov, "tp", axis=1, tiled=True)
    gram = lax.psum(
        lax.dot_general(
            rows, rows, (((0,), (0,)), ((), ())),
            precision=lax.Precision.HIGH, preferred_element_type=jnp.float32,
        ),
        "dp",
    )
    inverse_norm = 1.0 / (jnp.sqrt(jnp.trace(gram)) + NORM_EPS)
    square = gram * (inverse_norm * inverse_norm)
    first = lax.axis_index("tp") * width
    eye = (lax.broadcasted_iota(jnp.int32, (FF, width), 0) == lax.broadcasted_iota(jnp.int32, (FF, width), 1) + first).astype(jnp.float32)

    def mix(block):
        once = mm(square, block)
        return COEF_A * block + COEF_B * once + COEF_C * mm(square, once)

    def next_gram(block):
        return mix(mm(square, mix(block)))

    own = lax.dynamic_slice_in_dim(square, first, width, 1)
    mixed = COEF_A * eye + COEF_B * own + COEF_C * mm(square, own)
    gram_one = mix(mm(square, mixed))
    mixed_one = COEF_A * eye + COEF_B * gram_one + COEF_C * next_gram(gram_one)
    total = mix(mixed_one)
    result = mm(rows * inverse_norm, total)
    update = 0.2 * math.sqrt(max(D, FF)) * result
    new_weights = weights - LEARN_RATE * (update + WEIGHT_DECAY * weights)
    return (update, new_weights, new_momentum)


def solution(mesh):
    return jax.shard_map(
        on_device,
        mesh=mesh,
        in_specs=(P("dp", None, "tp"), P("dp", "tp"), P("dp", "tp")),
        out_specs=(P("dp", "tp"), P("dp", "tp"), P("dp", "tp")),
        check_vma=False,
    )
```

time: 1860 us -> 1140 us (0.61)
  waiting for transfers between devices: 1780 us -> 1080 us
  matrix products: 50.3 us -> 25.8 us
    psum x2 -> x1, waiting for transfers between devices: 1400 us -> 699 us  [on_device(): lax.psum(lax.dot_general(rows, rows, (((0,), (0,)), ((), ())), precision=...]
    dot_general x6 -> x13, matrix products: 50.3 us -> 25.8 us  [the longest x12 22 us: mm(): jnp.dot(left, right, precision=lax.Precision.HIGH, preferred_element_type...]
  transfers between devices with their start and end apart: 3 -> 2, of which waited for: 3 -> 2; matrix products, arithmetic and copies ran while one was open for 0% -> 0% of each run, Pallas kernels for 0% -> 0%
where the time goes in v1:
time: 1140 us
  waiting for transfers between devices  1080 us (95%)
  matrix products  25.8 us (2%)
  between operations  14.9 us (1%)
  other arithmetic  12.7 us (1%)
    psum x1, waiting for transfers between devices, on_device(): lax.psum(lax.dot_general(rows, rows, (((0,), (0,)), ((), ())), precision=...  699 us
    reduce_scatter x1, waiting for transfers between devices, on_device(): lax.psum_scatter(partials[0].astype(jnp.float32), 'dp', scatter_dimension...  380 us
  transfers between devices with their start and end apart: 2, of which 2 were waited for; matrix products, arithmetic and copies ran while one was open for 0% of the time, Pallas kernels for 0%

profile of v1, /device:TPU:8, one launch (start us, length us, event | category | flops | bytes accessed | tf_op | source)
XLA Modules:
  0.0 1138.1 jit_solution(6077524194569364086)
XLA Ops:
  7.2 0.0 reduce-scatter.2.cloned.1.call-start
  7.2 5.6 bitcast_convert_fusion
  12.8 0.0 copy-start
  12.8 0.0 reduce-scatter.2.cloned.1.call-update
  12.8 0.0 all-reduce.2.cloned.1.call-start
  12.9 379.5 %reduce-scatter.2.cloned.1.call-done = f32[112,256]{1,0:T(8,128)} async-done(((f32[7168,256]{1,0:T(8,128)}), f32[112,256]{1,0:T(8,128)}) %reduce-scatter.2.cloned.1.call-update) | async-done | bytes 114704 | tf_op jit(solution)/shard_map/reduce_scatter | solution.py:25
  392.4 0.0 copy-done
  392.4 1.6 multiply_add_fusion
  394.0 6.4 all_gather.3
  400.3 3.8 fusion.11
  404.1 0.0 all-reduce.2.cloned.1.call-update
  404.2 698.7 %all-reduce.2.cloned.1.call-done = f32[1024,1024]{1,0:T(8,128)} async-done(((f32[1024,1024]{1,0:T(8,128)}), f32[1024,1024]{1,0:T(8,128)}) %all-reduce.2.cloned.1.call-update) | async-done | bytes 4194320 | tf_op jit(solution)/shard_map/psum | solution.py:30
  1102.9 2.9 select_reduce_fusion
  1106.5 2.6 broadcast_multiply_fusion
  1109.2 1.9 fusion.5
  1111.1 1.9 fusion.12
  1112.9 1.8 fusion.13
  1114.8 1.9 fusion.4
  1116.7 1.9 fusion.14
  1118.5 2.1 fusion.3
  1120.7 1.8 fusion.15
  1122.5 1.8 fusion.16
  1124.3 2.1 fusion.6
  1126.4 1.8 fusion.17
  1128.2 0.0 copy-start.1
  1128.2 1.9 fusion
  1130.1 0.0 copy-done.1
  1130.1 1.1 multiply_subtract_fusion
  (1 shorter events, 0.0 us)
Async XLA Ops:
  7.2 385.2 %reduce-scatter.2.cloned.1.call-start = ((), (), s32[]{:S(2)}) async-start(), calls=%async_computation.1 | async-start | bytes 7454720 | tf_op jit(solution)/shard_map/reduce_scatter | solution.py:25
  12.8 379.6 %copy-start = (f32[112,256]{1,0:T(8,128)S(1)}, f32[112,256]{1,0:T(8,128)}, u32[]{:S(2)}) copy-start(f32[112,256]{1,0:T(8,128)} %param.4) | copy-start | bytes 344068
  12.8 1090.1 %all-reduce.2.cloned.1.call-start = ((), (), s32[]{:S(2)}) async-start(), calls=%async_computation.2 | async-start | bytes 8388608 | tf_op jit(solution)/shard_map/psum | solution.py:30
  1128.2 2.0 copy-start.1
Sparse Core Ops, SparseCore 0:
  12.9 379.4 reduce-scatter.1
  404.3 698.5 all-reduce.1

commit v2 on v1

v2 whole, which is shorter than its diff:
```python
import functools
import math

import jax
import jax.numpy as jnp
from jax import lax
from jax.experimental import pallas as pl
from jax.experimental.pallas import tpu as pltpu
from jax.sharding import PartitionSpec as P

MESH = pl.DeviceIdType.MESH
F32 = jnp.float32
NX, NY, NZ = 4, 2, 8
ROWS = 112
HEAD = 48
TAIL = ROWS - HEAD
W = 256
FAR = (2, 3, 4, 5, 6)
NEAR = (7, 0, 1)
D = 7168
FF = 1024
COEF_A = 3.4445
COEF_B = -4.775
COEF_C = 2.0315
MOMENTUM_DECAY = 0.95
LEARN_RATE = 0.02
WEIGHT_DECAY = 0.1
NORM_EPS = 1e-07


class Ring:
    def __init__(self, n, place, send, recv, send_sem, recv_sem):
        self.n, self.place, self.send, self.recv = n, place, send, recv
        self.send_sem, self.recv_sem = send_sem, recv_sem

    def copy(self, d, k):
        return pltpu.make_async_remote_copy(
            src_ref=self.send.at[d, k], dst_ref=self.recv.at[d, k],
            send_sem=self.send_sem.at[d, k], recv_sem=self.recv_sem.at[d, k],
            device_id=self.place(1 if d == 0 else -1), device_id_type=MESH,
        )

    def offset(self, d, k):
        return (1 if d == 0 else -1) * (self.n // 2 - (k + 1) // 2)

    def issue(self, k, own):
        for d in range(2):
            value = own(self.offset(d, k), (k + d) % 2)
            if k >= 2:
                value = value + self.recv[d, k - 2]
            self.send[d, k] = value
            self.copy(d, k).start()

    def arrive(self, k):
        for d in range(2):
            self.copy(d, k).wait_recv()

    def sent(self):
        for d in range(2):
            for k in range(self.n - 1):
                self.copy(d, k).wait_send()


class ShortRing:
    def __init__(self, n, place, sign, own, send, recv, send_sem, recv_sem):
        self.n, self.place, self.sign, self.own = n, place, sign, own
        self.send, self.recv, self.send_sem, self.recv_sem = send, recv, send_sem, recv_sem

    def copy(self, d, k):
        return pltpu.make_async_remote_copy(
            src_ref=self.send.at[d, k], dst_ref=self.recv.at[d, k],
            send_sem=self.send_sem.at[d, k], recv_sem=self.recv_sem.at[d, k],
            device_id=self.place(self.sign if d == 0 else -self.sign), device_id_type=MESH,
        )

    def issue(self, d, k):
        value = self.own((self.sign if d == 0 else -self.sign) * (self.n // 2 - k))
        if k > d:
            value = value + self.recv[d, k - 1]
        self.send[d, k] = value
        self.copy(d, k).start()

    def start(self):
        self.issue(0, 0)
        self.issue(1, 1)

    def arrive(self, d, k):
        self.copy(d, k).wait_recv()

    def step(self, k):
        for d in range(2):
            if k >= d:
                self.arrive(d, k)
                if k + 1 < self.n // 2:
                    self.issue(d, k + 1)

    def total(self):
        return self.own(0) + self.recv[0, self.n // 2 - 1] + self.recv[1, self.n // 2 - 1]

    def sent(self):
        for d in range(2):
            for k in range(d, self.n // 2):
                self.copy(d, k).wait_send()


def split(value):
    high = value.astype(jnp.bfloat16)
    return high, (value - high.astype(F32)).astype(jnp.bfloat16)


def cross(left, right):
    (lh, ll), (rh, rl) = split(left), split(right)
    dims = (((0,), (0,)), ((), ()))
    dot = functools.partial(lax.dot_general, dimension_numbers=dims, preferred_element_type=F32)
    return dot(lh, rh) + (dot(lh, rl) + dot(ll, rh))


def kernel(part_hbm, mom_ref, newm_ref, xg, gp, gq, part, fin, yrecv, acc_p, acc_q,
           p_send, p_recv, p2_send, p2_recv, qa_send, qa_recv, qb_send, qb_recv, q2_send, q2_recv,
           src_p, src_q, gacc_p, gacc_q, piece, yrecv2,
           gp1_send, gp1_recv, gp2_send, gp2_recv, gq1_send, gq1_recv, gq2_send, gq2_recv,
           load_sem, p_s, p_r, p2_s, p2_r, qa_s, qa_r, qb_s, qb_r, q2_s, q2_r, y_sems,
           x_s, x_r, gp1_s, gp1_r, gp2_s, gp2_r, gq1_s, gq1_r, gq2_s, gq2_r,
           ap_s, ap_r, aq_s, aq_r, az_s, az_r, ax_s, ax_r, cp_s, cp_r, cq_s, cq_r):
    dp = lax.axis_index("dp")
    tp = lax.axis_index("tp")
    x, yh, z = dp // 16, (dp // 8) % 2, dp % 8

    def at(xx, yy, zz):
        return (lax.rem(xx + 2 * NX, NX) * 16 + lax.rem(yy + NY, NY) * 8 + lax.rem(zz + 2 * NZ, NZ), tp)

    def along_z(step):
        return at(x, yh, z + step)

    def along_x(step):
        return at(x + step, yh, z)

    load = pltpu.make_async_copy(part_hbm, part, load_sem)
    load.start()
    peers = [(at(x + dx, yh, z)[0], tp_to) for dx in range(NX) for tp_to in (tp, tp ^ 2) if dx or tp_to is not tp]
    peers += [(at(x, yh, z + dz)[0], tp_to) for dz in range(1, NZ) for tp_to in (tp, tp ^ 2)]
    peers += [at(x, yh + 1, z), (dp, tp ^ 1), (dp, tp ^ 3)]
    barrier = pltpu.get_barrier_semaphore()
    for peer in peers:
        pl.semaphore_signal(barrier, inc=1, device_id=peer, device_id_type=MESH)
    load.wait()
    pl.semaphore_wait(barrier, len(peers))

    p1 = Ring(NZ, along_z, p_send, p_recv, p_s, p_r)
    p2 = Ring(NX, along_x, p2_send, p2_recv, p2_s, p2_r)
    qa = Ring(NX, along_x, qa_send, qa_recv, qa_s, qa_r)
    qb = Ring(NX, along_x, qb_send, qb_recv, qb_s, qb_r)
    q2 = Ring(NZ, along_z, q2_send, q2_recv, q2_s, q2_r)

    def dest(xx, yy, zz):
        return lax.rem(xx + NX, NX) * 16 + yy * 8 + lax.rem(zz + NZ, NZ)

    def own_p1(off, half):
        return jnp.stack([part[dest(xx, half, z + off), :HEAD, :].astype(F32) for xx in range(NX)])

    def own_p2(off, half):
        return acc_p[half, lax.rem(x + off + NX, NX)]

    def own_q(rels):
        def own(off, half):
            return jnp.stack([part[dest(x + off, half, z + rel), HEAD:, :].astype(F32) for rel in rels])
        return own

    own_qa, own_qb = own_q(FAR), own_q(NEAR)

    def own_q2(off, half):
        return acc_q[half, off % NZ]

    def p1_final():
        for half in range(2):
            acc_p[half] = own_p1(0, half) + p_recv[0, 5 + (half + 1) % 2] + p_recv[1, 5 + half]

    def p2_final():
        for half in range(2):
            fin[half, :HEAD] = own_p2(0, half) + p2_recv[0, 1 + (half + 1) % 2] + p2_recv[1, 1 + half]

    def q_final(rels, own, recv):
        first = rels[0]
        for half in range(2):
            value = own(0, half) + recv[0, 1 + (half + 1) % 2] + recv[1, 1 + half]
            for i, rel in enumerate(rels):
                acc_q[half, rel] = value[i]

    def q2_final():
        for half in range(2):
            fin[half, HEAD:] = own_q2(0, half) + q2_recv[0, 5 + (half + 1) % 2] + q2_recv[1, 5 + half]

    p1.issue(0, own_p1)
    qa.issue(0, own_qa)
    p1.issue(1, own_p1)
    qa.issue(1, own_qa)
    p1.arrive(0)
    p1.issue(2, own_p1)
    qa.arrive(0)
    qa.issue(2, own_qa)
    p1.arrive(1)
    p1.issue(3, own_p1)
    p1.arrive(2)
    p1.issue(4, own_p1)
    qa.arrive(1)
    qb.issue(0, own_qb)
    p1.arrive(3)
    p1.issue(5, own_p1)
    qa.arrive(2)
    qb.issue(1, own_qb)
    q_final(FAR, own_qa, qa_recv)
    p1.arrive(4)
    p1.issue(6, own_p1)
    q2.issue(0, own_q2)
    q2.issue(1, own_q2)
    qb.arrive(0)
    qb.issue(2, own_qb)
    p1.arrive(5)
    q2.arrive(0)
    q2.issue(2, own_q2)
    p1.arrive(6)
    p1_final()
    p2.issue(0, own_p2)
    p2.issue(1, own_p2)
    q2.arrive(1)
    q2.issue(3, own_q2)
    qb.arrive(1)
    q2.arrive(2)
    q2.issue(4, own_q2)
    qb.arrive(2)
    q_final(NEAR, own_qb, qb_recv)
    q2.arrive(3)
    q2.issue(5, own_q2)
    q2.arrive(4)
    q2.issue(6, own_q2)
    p2.arrive(0)
    p2.issue(2, own_p2)
    p2.arrive(1)
    p2.arrive(2)
    p2_final()
    q2.arrive(5)
    q2.arrive(6)
    q2_final()


    def remote(src, dst, send_sem, recv_sem, device):
        return pltpu.make_async_remote_copy(
            src_ref=src, dst_ref=dst, send_sem=send_sem, recv_sem=recv_sem, device_id=device, device_id_type=MESH,
        )

    swap = remote(fin.at[1 - yh], yrecv, y_sems.at[0], y_sems.at[1], at(x, yh + 1, z))
    swap.start()
    for ring in (p1, p2, qa, qb, q2):
        ring.sent()
    swap.wait()
    gradient = fin[yh] + yrecv[...]
    new_momentum = MOMENTUM_DECAY * mom_ref[...] + gradient
    newm_ref[...] = new_momentum
    xg[tp] = gradient + MOMENTUM_DECAY * new_momentum

    gather = [remote(xg.at[tp], xg.at[tp], x_s.at[m - 1], x_r.at[m - 1], (dp, tp ^ m)) for m in (1, 2, 3)]
    gather[1].start()
    gather[2].start()
    gather[0].start()

    own_x = xg[tp]
    diag = cross(own_x, own_x)
    src_p[0] = diag[:, :128]
    src_p[1] = diag[:, 128:]
    for copy in gather:
        copy.wait_recv()
    side = cross(xg[lax.rem(tp + 1, 4)], own_x)
    high_x = xg[tp % 2 + 2]
    left = jnp.where(tp < 2, high_x[:, :128], high_x[:, 128:])
    far = cross(left, xg[tp % 2])
    for c in range(2):
        src_q[c, :256] = side[:, 128 * c:128 * c + 128]
        src_q[c, 256:] = far[:, 128 * c:128 * c + 128]

    def rows_of(xx, zz, rows):
        return pl.ds(pl.multiple_of(((xx % 2) * 8 + zz) * rows, 8), rows)

    def own_gp1(off):
        zz = lax.rem(z + off + NZ, NZ)
        return jnp.stack([src_p[xx // 2, rows_of(xx, zz, 16), :] for xx in range(NX)])

    def own_gq1(off):
        xx = lax.rem(x + off + NX, NX)
        return jnp.stack([src_q[xx // 2, rows_of(xx, zz, 24), :] for zz in range(NZ)])

    def own_gp2(off):
        return gacc_p[lax.rem(x + off + NX, NX)]

    def own_gq2(off):
        return gacc_q[lax.rem(z + off + NZ, NZ)]

    gp1 = ShortRing(NZ, along_z, 1, own_gp1, gp1_send, gp1_recv, gp1_s, gp1_r)
    gp2 = ShortRing(NX, along_x, -1, own_gp2, gp2_send, gp2_recv, gp2_s, gp2_r)
    gq1 = ShortRing(NX, along_x, 1, own_gq1, gq1_send, gq1_recv, gq1_s, gq1_r)
    gq2 = ShortRing(NZ, along_z, -1, own_gq2, gq2_send, gq2_recv, gq2_s, gq2_r)

    gp1.start()
    gq1.start()
    gp1.step(0)
    gq1.step(0)
    gp1.step(1)
    gq1.step(1)
    gacc_q[...] = gq1.total()
    gq2.start()
    gp1.step(2)
    gq2.step(0)
    gp1.step(3)
    gacc_p[...] = gp1.total()
    gp2.start()
    gq2.step(1)
    gp2.step(0)
    gq2.step(2)
    gp2.step(1)
    gq2.step(3)
    piece[:16] = gp2.total()
    piece[16:] = gq2.total()
    swap2 = remote(piece, yrecv2, y_sems.at[2], y_sems.at[3], at(x, yh + 1, z))
    swap2.start()
    for ring in (gp1, gp2, gq1, gq2):
        ring.sent()
    for copy in gather:
        copy.wait_send()
    swap2.wait()

    lo, core = tp // 2, tp % 2
    sibling = (dp, tp ^ 1)
    gp[core, z, x, lo] = piece[:16] + yrecv2[:16]
    gq[core, x, z, lo] = piece[16:] + yrecv2[16:]

    near_p, near_q = [], []
    for dy in range(2):
        for dx in range(NX):
            if dx or dy:
                mine = gp.at[core, z, x, lo]
                i = dy * NX + dx
                near_p.append(remote(mine, mine, ap_s.at[i], ap_r.at[i], (at(x + dx, yh, z)[0], tp ^ (2 * dy))))
        for dz in range(NZ):
            if dz or dy:
                mine = gq.at[core, x, z, lo]
                i = dy * NZ + dz
                near_q.append(remote(mine, mine, aq_s.at[i], aq_r.at[i], (at(x, yh, z + dz)[0], tp ^ (2 * dy))))
    for copy in near_p + near_q:
        copy.start()

    def z_at(off):
        return lax.rem(z + off + NZ, NZ)

    def x_at(off):
        return lax.rem(x + off + NX, NX)

    def pass_z(d, hop):
        sign = 1 if d == 0 else -1
        chunk = gp.at[core, z_at(-sign * hop)]
        if hop == 3:
            chunk = chunk.at[pl.ds(2 * d, 2)]
        return remote(chunk, chunk, az_s.at[d, hop], az_r.at[d, hop], along_z(sign))

    def pass_x(d, part_at):
        sign = 1 if d == 0 else -1
        half = d if part_at != 1 else 1 - d
        chunk = gq.at[core, x if part_at < 2 else x_at(-sign), pl.ds(4 * half, 4)]
        return remote(chunk, chunk, ax_s.at[d, part_at], ax_r.at[d, part_at], along_x(sign))

    shared = []

    def share_p(off, first=0, count=NX):
        i = len(shared)
        chunk = gp.at[core, z_at(off), pl.ds(first, count)]
        shared.append((chunk, remote(chunk, chunk, cp_s.at[i], cp_r.at[i], sibling)))
        shared[-1][1].start()

    def share_q(off, half):
        i = len(shared)
        chunk = gq.at[core, x_at(off), pl.ds(4 * half, 4)]
        shared.append((chunk, remote(chunk, chunk, cp_s.at[i], cp_r.at[i], sibling)))
        shared[-1][1].start()

    for copy in near_p:
        copy.wait_recv()
    for d in range(2):
        pass_z(d, 0).start()
    share_p(0)
    for copy in near_q:
        copy.wait_recv()
    for d in range(2):
        pass_x(d, 0).start()
    for d in range(2):
        pass_x(d, 1).start()
    share_q(0, 0)
    share_q(0, 1)

    def z_step(hop):
        for d in range(2):
            pass_z(d, hop).wait_recv()
            if hop < 3:
                pass_z(d, hop + 1).start()
        for d in range(2):
            sign = 1 if d == 0 else -1
            if hop < 3:
                share_p(-sign * (hop + 1))
            else:
                share_p(4, 2 * d, 2)

    def x_step(part_at):
        for d in range(2):
            pass_x(d, part_at).wait_recv()
            if part_at == 0:
                pass_x(d, 2).start()
        for d in range(2):
            sign = 1 if d == 0 else -1
            half = d if part_at != 1 else 1 - d
            share_q(-sign if part_at < 2 else 2, half)

    z_step(0)
    z_step(1)
    x_step(0)
    z_step(2)
    x_step(1)
    z_step(3)
    x_step(2)
    for _, copy in shared:
        copy.wait()
    for copy in near_p + near_q:
        copy.wait_send()
    for d in range(2):
        for hop in range(4):
            pass_z(d, hop).wait_send()
        for part_at in range(3):
            pass_x(d, part_at).wait_send()


def communicate(partials, momentum):
    def ring(n, *block):
        return [pltpu.VMEM((2, n - 1) + block, F32)] * 2

    def short(n, *block):
        return [pltpu.VMEM((2, n // 2) + block, F32)] * 2

    def sems(*shape):
        return [pltpu.SemaphoreType.DMA(shape)] * 2

    vmem = pl.BlockSpec(memory_space=pltpu.VMEM)
    return pl.pallas_call(
        kernel,
        out_shape=[
            jax.ShapeDtypeStruct((ROWS, W), F32),
            jax.ShapeDtypeStruct((4, ROWS, W), F32),
            jax.ShapeDtypeStruct((2, NZ, NX, 2, 16, 128), F32),
            jax.ShapeDtypeStruct((2, NX, NZ, 2, 24, 128), F32),
        ],
        in_specs=[pl.BlockSpec(memory_space=pl.ANY), vmem],
        out_specs=[vmem] * 4,
        scratch_shapes=[
            pltpu.VMEM((64, ROWS, W), jnp.bfloat16),
            pltpu.VMEM((2, ROWS, W), F32),
            pltpu.VMEM((ROWS, W), F32),
            pltpu.VMEM((2, NX, HEAD, W), F32),
            pltpu.VMEM((2, NZ, TAIL, W), F32),
            *ring(NZ, NX, HEAD, W), *ring(NX, HEAD, W),
            *ring(NX, len(FAR), TAIL, W), *ring(NX, len(NEAR), TAIL, W), *ring(NZ, TAIL, W),
            pltpu.VMEM((2, 256, 128), F32), pltpu.VMEM((2, 384, 128), F32),
            pltpu.VMEM((NX, 16, 128), F32), pltpu.VMEM((NZ, 24, 128), F32),
            pltpu.VMEM((40, 128), F32), pltpu.VMEM((40, 128), F32),
            *short(NZ, NX, 16, 128), *short(NX, 16, 128), *short(NX, NZ, 24, 128), *short(NZ, 24, 128),
            pltpu.SemaphoreType.DMA,
            *sems(2, NZ - 1), *sems(2, NX - 1), *sems(2, NX - 1), *sems(2, NX - 1), *sems(2, NZ - 1),
            pltpu.SemaphoreType.DMA((4,)),
            *sems(3),
            *sems(2, NZ // 2), *sems(2, NX // 2), *sems(2, NX // 2), *sems(2, NZ // 2),
            *sems(2 * NX), *sems(2 * NZ), *sems(2, 4), *sems(2, 3), *sems(18), *sems(1),
        ],
        compiler_params=pltpu.CompilerParams(collective_id=0, has_side_effects=True, vmem_limit_bytes=52 * 1024 * 1024),
    )(partials.reshape(64, ROWS, W), momentum)


def finish(x_ref, gp, gq, w_ref, m_ref, update_ref, neww_ref, newm_ref,
           a, a2, low, ah, al, a2h, a2l, mh, ml, vh, vl, y, w):
    tp = lax.axis_index("tp")
    newm_ref[...] = m_ref[...]
    trace = jnp.zeros((1, 1), F32)
    for t in range(4):
        core, lo, base = t % 2, t // 2, 256 * t
        for xx in range(NX):
            for zz in range(NZ):
                r, c = (xx % 2) * 8 + zz, xx // 2
                a[base + 16 * r:base + 16 * r + 16, base + 128 * c:base + 128 * c + 128] = gp[core, zz, xx, lo]
                low[t, 24 * r:24 * r + 24, 128 * c:128 * c + 128] = gq[core, xx, zz, lo]
        block = a[base:base + 256, base:base + 256]
        on_diag = lax.broadcasted_iota(jnp.int32, (256, 256), 0) == lax.broadcasted_iota(jnp.int32, (256, 256), 1)
        trace = trace + jnp.sum(jnp.where(on_diag, block, 0.0), keepdims=True)
    for t in range(4):
        nxt = (t + 1) % 4
        side = low[t, :256, :]
        a[256 * nxt:256 * nxt + 256, 256 * t:256 * t + 256] = side
        a[256 * t:256 * t + 256, 256 * nxt:256 * nxt + 256] = side.T
        far = low[t, 256:, :]
        i, j = 256 * (t % 2 + 2) + 128 * (t // 2), 256 * (t % 2)
        a[i:i + 128, j:j + 256] = far
        a[j:j + 256, i:i + 128] = far.T
    inverse = 1.0 / (jnp.sqrt(trace) + NORM_EPS)
    scale = inverse * inverse

    def tiles(body):
        def step(i, carry):
            body(pl.ds(pl.multiple_of(i * 256, 256), 256), i)
            return carry
        lax.fori_loop(0, 4, step, 0)

    def prepare(rows, _):
        block = a[rows, :] * scale
        a[rows, :] = block
        ah[rows, :], al[rows, :] = split(block)

    tiles(prepare)

    def dot3(lh, ll, rh, rl):
        dot = functools.partial(jnp.dot, preferred_element_type=F32)
        return dot(lh, rh) + (dot(lh, rl) + dot(ll, rh))

    for i in range(4):
        rows = slice(256 * i, 256 * i + 256)
        for j in range(i, 4):
            cols = slice(256 * j, 256 * j + 256)
            block = dot3(ah[rows, :], al[rows, :], ah[:, cols], al[:, cols])
            a2[rows, cols] = block
            if j > i:
                a2[cols, rows] = block.T

    def mix(rows, i):
        square = a2[rows, :]
        a2h[rows, :], a2l[rows, :] = split(square)
        same = lax.broadcasted_iota(jnp.int32, (256, FF), 0) + i * 256 == lax.broadcasted_iota(jnp.int32, (256, FF), 1)
        value = COEF_B * a[rows, :] + COEF_C * square + jnp.where(same, COEF_A, 0.0)
        mh[rows, :], ml[rows, :] = split(value)

    tiles(mix)

    own = pl.ds(pl.multiple_of(tp * 256, 256), 256)

    def eye(i):
        return jnp.where(
            lax.broadcasted_iota(jnp.int32, (256, W), 0) + i * 256 == lax.broadcasted_iota(jnp.int32, (256, W), 1) + tp * 256,
            COEF_A, 0.0,
        )

    def start(rows, i):
        w[rows, :] = a[rows, own]
        value = COEF_B * a[rows, own] + COEF_C * a2[rows, own] + eye(i)
        vh[rows, :], vl[rows, :] = split(value)

    tiles(start)

    def product(high, lowp, after):
        def body(rows, i):
            y[rows, :] = after(dot3(high[rows, :], lowp[rows, :], vh[...], vl[...]), rows, i)
        tiles(body)

        def again(rows, i):
            vh[rows, :], vl[rows, :] = split(y[rows, :])
        tiles(again)

    product(mh, ml, lambda value, rows, i: value)
    product(a2h, a2l, lambda value, rows, i: COEF_B * w[rows, :] + COEF_C * value)
    product(mh, ml, lambda value, rows, i: value)
    product(mh, ml, lambda value, rows, i: value + eye(i))

    xh, xl = split(jnp.concatenate([x_ref[t] for t in range(4)], axis=1) * inverse)
    result = jnp.zeros((ROWS, W), F32)
    for t in range(4):
        cols = slice(256 * t, 256 * t + 256)
        once_h, once_l = split(dot3(xh, xl, mh[:, cols], ml[:, cols]))
        result = result + dot3(once_h, once_l, vh[cols, :], vl[cols, :])
    update = 0.2 * math.sqrt(max(D, FF)) * result
    update_ref[...] = update
    neww_ref[...] = w_ref[...] - LEARN_RATE * (update + WEIGHT_DECAY * w_ref[...])


def orthogonalize(x, gp, gq, weights, new_momentum):
    vmem = pl.BlockSpec(memory_space=pltpu.VMEM)
    block = jax.ShapeDtypeStruct((ROWS, W), F32)
    half = jnp.bfloat16
    return pl.pallas_call(
        finish,
        out_shape=[block] * 3,
        in_specs=[vmem] * 5,
        out_specs=[vmem] * 3,
        scratch_shapes=[
            pltpu.VMEM((FF, FF), F32), pltpu.VMEM((FF, FF), F32), pltpu.VMEM((4, 384, W), F32),
            *[pltpu.VMEM((FF, FF), half)] * 6,
            pltpu.VMEM((FF, W), half), pltpu.VMEM((FF, W), half),
            pltpu.VMEM((FF, W), F32), pltpu.VMEM((FF, W), F32),
        ],
        compiler_params=pltpu.CompilerParams(vmem_limit_bytes=52 * 1024 * 1024),
    )(x, gp, gq, weights, new_momentum)


def on_device(partials, momentum, weights):
    new_momentum, x, gp, gq = communicate(partials[0], momentum)
    return tuple(orthogonalize(x, gp, gq, weights, new_momentum))


def solution(mesh):
    return jax.shard_map(
        on_device,
        mesh=mesh,
        in_specs=(P("dp", None, "tp"), P("dp", "tp"), P("dp", "tp")),
        out_specs=(P("dp", "tp"), P("dp", "tp"), P("dp", "tp")),
        check_vma=False,
    )
```

time: 1140 us -> 137 us (0.12)
  the two profiles are of different devices: /device:TPU:8 before, /device:TPU:1 now
where the time goes in v2:
time: 137 us; the launch traced here: 136 us
  Pallas kernels  134 us (98%)
    pallas_call x1, Pallas kernels, communicate(): pl.pallas_call(kernel, out_shape=[jax.ShapeDtypeStruct((ROWS, W), F32), j...  112 us
    pallas_call x1, Pallas kernels, orthogonalize(): pl.pallas_call(finish, out_shape=[block] * 3, in_specs=[vmem] * 5, out_sp...  22.5 us

profile of v2, /device:TPU:1, one launch (start us, length us, event | category | flops | bytes accessed | tf_op | source)
XLA Modules:
  0.0 136.0 jit_solution(16980597232952518384)
XLA Ops:
  0.6 0.0 copy-start
  0.6 0.0 copy-start.1
  0.7 0.9 copy-done.1
  1.6 111.9 %shard_map.58 = (f32[112,256]{1,0:T(8,128)S(1)}, f32[4,112,256]{2,1,0:T(8,128)S(1)}, f32[2,8,4,2,16,128]{5,4,3,2,1,0:T(8,128)S(1)}, f32[2,4,8,2,24,128]{5,4,3,2,1,0:T(8,128)}) custom-call(bf16[64,112,256]{2,1,0:T(8,128)(2,1)} %bitcast.1, f32[112,256]{1,0:T(8,128)S(1)} %copy-done.1), custom_call_target="tpu_custom_call" | custom-call | tf_op jit(solution)/shard_map/pallas_call | solution.py:448
  113.5 0.0 copy-done
  113.5 22.5 %shard_map.59 = (f32[112,256]{1,0:T(8,128)}, f32[112,256]{1,0:T(8,128)}, f32[112,256]{1,0:T(8,128)}) custom-call(f32[4,112,256]{2,1,0:T(8,128)S(1)} %get-tuple-element.7.x_ref, f32[2,8,4,2,16,128]{5,4,3,2,1,0:T(8,128)S(1)} %get-tuple-element.8.gp, f32[2,4,8,2,24,128]{5,4,3,2,1,0:T(8,128)} %get-tuple-element.9.gq, f32[112,256]{1,0:T(8,128)S(1)} %copy-done, ...), custom_call_target="tpu_custom_call" | custom-call | tf_op jit(solution)/shard_map/pallas_call | solution.py:587
Async XLA Ops:
  0.6 112.8 %copy-start = (f32[112,256]{1,0:T(8,128)S(1)}, f32[112,256]{1,0:T(8,128)}, u32[]{:S(2)}) copy-start(f32[112,256]{1,0:T(8,128)} %w_ref.1) | copy-start | bytes 344068
  0.6 0.9 copy-start.1

commit v3 on v2

v3 whole, which is shorter than its diff:
```python
import functools
import math

import jax
import jax.numpy as jnp
from jax import lax
from jax.experimental import pallas as pl
from jax.experimental.pallas import tpu as pltpu
from jax.sharding import PartitionSpec as P

MESH = pl.DeviceIdType.MESH
F32 = jnp.float32
NX, NY, NZ = 4, 2, 8
ROWS = 112
HEAD = 48
TAIL = ROWS - HEAD
W = 256
FAR = (2, 3, 4, 5, 6)
MID = (7, 1)
NEAR = (0,)
D = 7168
FF = 1024
COEF_A = 3.4445
COEF_B = -4.775
COEF_C = 2.0315
MOMENTUM_DECAY = 0.95
LEARN_RATE = 0.02
WEIGHT_DECAY = 0.1
NORM_EPS = 1e-07
NESTEROV_GRAD = 1.0 + MOMENTUM_DECAY


class Ring:
    def __init__(self, n, place, send, recv, send_sem, recv_sem):
        self.n, self.place, self.send, self.recv = n, place, send, recv
        self.send_sem, self.recv_sem = send_sem, recv_sem

    def copy(self, d, k):
        return pltpu.make_async_remote_copy(
            src_ref=self.send.at[d, k], dst_ref=self.recv.at[d, k],
            send_sem=self.send_sem.at[d, k], recv_sem=self.recv_sem.at[d, k],
            device_id=self.place(1 if d == 0 else -1), device_id_type=MESH,
        )

    def offset(self, d, k):
        return (1 if d == 0 else -1) * (self.n // 2 - (k + 1) // 2)

    def issue(self, k, own):
        for d in range(2):
            value = own(self.offset(d, k), (k + d) % 2)
            if k >= 2:
                value = value + self.recv[d, k - 2]
            self.send[d, k] = value
            self.copy(d, k).start()

    def arrive(self, k):
        for d in range(2):
            self.copy(d, k).wait_recv()

    def sent(self):
        for d in range(2):
            for k in range(self.n - 1):
                self.copy(d, k).wait_send()


def split(value):
    high = value.astype(jnp.bfloat16)
    return high, (value - high.astype(F32)).astype(jnp.bfloat16)


def cross(left, right):
    (lh, ll), (rh, rl) = split(left), split(right)
    dims = (((0,), (0,)), ((), ()))
    dot = functools.partial(lax.dot_general, dimension_numbers=dims, preferred_element_type=F32)
    return dot(lh, rh) + (dot(lh, rl) + dot(ll, rh))


def kernel(part_hbm, mom_ref, newm_ref, xg, gp, gq, part, fin, acc_p, acc_q,
           p_send, p_recv, p2_send, p2_recv, qa_send, qa_recv, qb_send, qb_recv, qc_send, qc_recv, q2_send, q2_recv,
           same_recv, side_send, side_recv, cross_send, cross_recv,
           src_p, src_q, one_p, one_q, tot_p, tot_q, two_p, two_q,
           load_sem, p_s, p_r, p2_s, p2_r, qa_s, qa_r, qb_s, qb_r, qc_s, qc_r, q2_s, q2_r, y_s, y_r,
           x_s, x_r, g1p_s, g1p_r, g1q_s, g1q_r, g2p_s, g2p_r, g2q_s, g2q_r,
           ap_s, ap_r, aq_s, aq_r, az_s, az_r, ax_s, ax_r, c_s, c_r):
    dp = lax.axis_index("dp")
    tp = lax.axis_index("tp")
    x, yh, z = dp // 16, (dp // 8) % 2, dp % 8
    lo, core = tp // 2, tp % 2
    sibling = (dp, tp ^ 1)
    pending = []

    def x_at(off):
        return lax.rem(x + off + 2 * NX, NX)

    def z_at(off):
        return lax.rem(z + off + 2 * NZ, NZ)

    def at(dx, dy, dz, other=0):
        return (x_at(dx) * 16 + lax.rem(yh + dy, NY) * 8 + z_at(dz), tp ^ (2 * other))

    def remote(src, dst, send_sem, recv_sem, device):
        return pltpu.make_async_remote_copy(
            src_ref=src, dst_ref=dst, send_sem=send_sem, recv_sem=recv_sem, device_id=device, device_id_type=MESH,
        )

    def begin(copy):
        copy.start()
        pending.append(copy)
        return copy

    def drain():
        for copy in pending:
            copy.wait_send()

    load = pltpu.make_async_copy(part_hbm, part, load_sem)
    load.start()
    peers = [at(dx, dy, 0, o) for dx in range(1, NX) for dy, o in ((0, 0), (1, 0), (0, 1))]
    peers += [at(0, dy, dz, o) for dz in range(1, NZ) for dy, o in ((0, 0), (1, 0), (0, 1))]
    peers += [at(0, 1, 0), at(0, 0, 0, 1), at(0, 1, 0, 1), sibling]
    barrier = pltpu.get_barrier_semaphore()
    for peer in peers:
        pl.semaphore_signal(barrier, inc=1, device_id=peer, device_id_type=MESH)
    load.wait()
    pl.semaphore_wait(barrier, len(peers))

    def along_z(step):
        return at(0, 0, step)

    def along_x(step):
        return at(step, 0, 0)

    p1 = Ring(NZ, along_z, p_send, p_recv, p_s, p_r)
    p2 = Ring(NX, along_x, p2_send, p2_recv, p2_s, p2_r)
    qa = Ring(NX, along_x, qa_send, qa_recv, qa_s, qa_r)
    qb = Ring(NX, along_x, qb_send, qb_recv, qb_s, qb_r)
    qc = Ring(NX, along_x, qc_send, qc_recv, qc_s, qc_r)
    q2 = Ring(NZ, along_z, q2_send, q2_recv, q2_s, q2_r)

    def own_p1(off, half):
        return jnp.stack([part[xx * 16 + half * 8 + z_at(off), :HEAD, :].astype(F32) for xx in range(NX)])

    def own_p2(off, half):
        return acc_p[half, x_at(off)]

    def own_q(rels):
        def own(off, half):
            return jnp.stack([part[x_at(off) * 16 + half * 8 + z_at(rel), HEAD:, :].astype(F32) for rel in rels])
        return own

    own_qa, own_qb, own_qc = own_q(FAR), own_q(MID), own_q(NEAR)

    def own_q2(off, half):
        return acc_q[half, off % NZ]

    def p1_final():
        for half in range(2):
            acc_p[half] = own_p1(0, half) + p_recv[0, 5 + (half + 1) % 2] + p_recv[1, 5 + half]

    def p2_final():
        for half in range(2):
            fin[half, :HEAD] = own_p2(0, half) + p2_recv[0, 1 + (half + 1) % 2] + p2_recv[1, 1 + half]

    def q_final(rels, own, recv):
        for half in range(2):
            value = own(0, half) + recv[0, 1 + (half + 1) % 2] + recv[1, 1 + half]
            for i, rel in enumerate(rels):
                acc_q[half, rel] = value[i]

    def q2_final():
        for half in range(2):
            fin[half, HEAD:] = own_q2(0, half) + q2_recv[0, 5 + (half + 1) % 2] + q2_recv[1, 5 + half]

    def columns_start(i):
        rows = pl.ds(0, HEAD) if i == 0 else pl.ds(HEAD, TAIL)
        begin(remote(fin.at[1 - yh, rows], same_recv.at[rows], y_s.at[0, i], y_r.at[0, i], at(0, 1, 0)))
        cross_send[rows] = NESTEROV_GRAD * fin[1 - yh, rows]
        begin(remote(cross_send.at[rows], cross_recv.at[rows], y_s.at[1, i], y_r.at[1, i], at(0, 1, 0, 1)))
        side_send[rows] = NESTEROV_GRAD * fin[yh, rows] + MOMENTUM_DECAY * MOMENTUM_DECAY * mom_ref[rows]
        begin(remote(side_send.at[rows], side_recv.at[rows], y_s.at[2, i], y_r.at[2, i], at(0, 0, 0, 1)))

    def columns_end(i):
        rows = pl.ds(0, HEAD) if i == 0 else pl.ds(HEAD, TAIL)
        for buf, j in ((same_recv, 0), (cross_recv, 1), (side_recv, 2)):
            remote(buf.at[rows], buf.at[rows], y_s.at[j, i], y_r.at[j, i], sibling).wait_recv()
        gradient = fin[yh, rows] + same_recv[rows]
        new_momentum = MOMENTUM_DECAY * mom_ref[rows] + gradient
        newm_ref[rows] = new_momentum
        xg[tp, rows] = gradient + MOMENTUM_DECAY * new_momentum
        xg[tp ^ 2, rows] = side_recv[rows] + cross_recv[rows]
        for j, slot in enumerate((tp, tp ^ 2)):
            mine = xg.at[slot, rows]
            begin(remote(mine, mine, x_s.at[j, i], x_r.at[j, i], sibling))

    def columns_wait(i):
        rows = pl.ds(0, HEAD) if i == 0 else pl.ds(HEAD, TAIL)
        for j, slot in enumerate((tp ^ 1, tp ^ 3)):
            other = xg.at[slot, rows]
            remote(other, other, x_s.at[j, i], x_r.at[j, i], sibling).wait_recv()

    p1.issue(0, own_p1)
    qa.issue(0, own_qa)
    p1.issue(1, own_p1)
    qa.issue(1, own_qa)
    p1.arrive(0)
    p1.issue(2, own_p1)
    qa.arrive(0)
    qa.issue(2, own_qa)
    p1.arrive(1)
    p1.issue(3, own_p1)
    p1.arrive(2)
    p1.issue(4, own_p1)
    qa.arrive(1)
    qb.issue(0, own_qb)
    qb.issue(1, own_qb)
    p1.arrive(3)
    p1.issue(5, own_p1)
    qa.arrive(2)
    qc.issue(0, own_qc)
    q_final(FAR, own_qa, qa_recv)
    q2.issue(0, own_q2)
    q2.issue(1, own_q2)
    p1.arrive(4)
    p1.issue(6, own_p1)
    qb.arrive(0)
    qb.issue(2, own_qb)
    q2.arrive(0)
    q2.issue(2, own_q2)
    q2.arrive(1)
    q2.issue(3, own_q2)
    qb.arrive(1)
    qc.issue(1, own_qc)
    p1.arrive(5)
    qb.arrive(2)
    q_final(MID, own_qb, qb_recv)
    qc.arrive(0)
    qc.issue(2, own_qc)
    p1.arrive(6)
    p1_final()
    p2.issue(0, own_p2)
    p2.issue(1, own_p2)
    q2.arrive(2)
    q2.issue(4, own_q2)
    q2.arrive(3)
    q2.issue(5, own_q2)
    q2.arrive(4)
    q2.issue(6, own_q2)
    p2.arrive(0)
    p2.issue(2, own_p2)
    qc.arrive(1)
    qc.arrive(2)
    q_final(NEAR, own_qc, qc_recv)
    p2.arrive(1)
    p2.arrive(2)
    p2_final()
    columns_start(0)
    q2.arrive(5)
    q2.arrive(6)
    q2_final()
    columns_start(1)
    columns_end(0)
    for ring in (p1, p2, qa, qb, qc, q2):
        ring.sent()
    columns_end(1)
    columns_wait(0)

    def place(block, rows):
        for xx in range(NX):
            for zz in range(NZ):
                r = rows * ((xx % 2) * 8 + zz)
                yield xx, zz, block[r:r + rows, 128 * (xx // 2):128 * (xx // 2) + 128]

    own_x = xg[tp]
    for xx, zz, value in place(cross(own_x, own_x), 16):
        src_p[zz, xx] = value
    rp = [(dz, remote(src_p.at[z_at(dz)], one_p.at[dz - 1], g1p_s.at[dz - 1], g1p_r.at[dz - 1], along_z(dz)))
          for dz in (4, 3, 5, 2, 6, 1, 7)]
    for _, copy in rp:
        begin(copy)
    columns_wait(1)
    high_x = xg[tp % 2 + 2]
    left = jnp.where(tp < 2, high_x[:, :128], high_x[:, 128:])
    lower = jnp.concatenate([cross(xg[lax.rem(tp + 1, 4)], own_x), cross(left, xg[tp % 2])], axis=0)
    for xx, zz, value in place(lower, 24):
        src_q[xx, zz] = value
    rq = [(dx, remote(src_q.at[x_at(dx)], one_q.at[dx - 1], g1q_s.at[dx - 1], g1q_r.at[dx - 1], along_x(dx)))
          for dx in (2, 1, 3)]
    for _, copy in rq:
        begin(copy)

    for _, copy in rp:
        copy.wait_recv()
    total = src_p[z]
    for i in range(NZ - 1):
        total = total + one_p[i]
    tot_p[...] = total
    second_p, second_q = [], []
    for dx in (2, 1, 3, 0):
        for dy in range(2):
            if dx or dy:
                i = dy * NX + dx
                second_p.append(begin(remote(tot_p.at[x_at(dx)], two_p.at[i], g2p_s.at[i], g2p_r.at[i], at(dx, dy, 0))))
    for _, copy in rq:
        copy.wait_recv()
    total = src_q[x]
    for i in range(NX - 1):
        total = total + one_q[i]
    tot_q[...] = total
    for dz in (4, 3, 5, 2, 6, 1, 7, 0):
        for dy in range(2):
            if dz or dy:
                i = dy * NZ + dz
                second_q.append(begin(remote(tot_q.at[z_at(dz)], two_q.at[i], g2q_s.at[i], g2q_r.at[i], at(0, dy, dz))))

    near_p, near_q = [], []
    for copy in second_p:
        copy.wait_recv()
    total = tot_p[x]
    for i in range(1, 2 * NX):
        total = total + two_p[i]
    mine = gp.at[core, z, x, lo]
    mine[...] = total
    for dx in (2, 1, 3, 0):
        for dy in range(2):
            if dx or dy:
                i = dy * NX + dx
                near_p.append(begin(remote(mine, mine, ap_s.at[i], ap_r.at[i], at(dx, 0, 0, dy))))
    for copy in second_q:
        copy.wait_recv()
    total = tot_q[z]
    for i in range(1, 2 * NZ):
        total = total + two_q[i]
    mine_q = gq.at[core, x, z, lo]
    mine_q[...] = total
    for dz in (4, 3, 5, 2, 6, 1, 7, 0):
        for dy in range(2):
            if dz or dy:
                i = dy * NZ + dz
                near_q.append(begin(remote(mine_q, mine_q, aq_s.at[i], aq_r.at[i], at(0, 0, dz, dy))))

    def pass_z(d, hop, sub):
        sign = 1 if d == 0 else -1
        chunk = gp.at[core, z_at(-sign * hop), pl.ds(2 * sub, 2)]
        return remote(chunk, chunk, az_s.at[d, hop, sub], az_r.at[d, hop, sub], along_z(sign))

    def pass_x(d, part_at):
        sign = 1 if d == 0 else -1
        half = d if part_at != 1 else 1 - d
        chunk = gq.at[core, x if part_at < 2 else x_at(-sign), pl.ds(4 * half, 4)]
        return remote(chunk, chunk, ax_s.at[d, part_at], ax_r.at[d, part_at], along_x(sign))

    shared = []

    def share(chunk):
        i = len(shared)
        shared.append(begin(remote(chunk, chunk, c_s.at[i], c_r.at[i], sibling)))

    for copy in near_p:
        copy.wait_recv()
    for turn in range(2):
        for d in range(2):
            begin(pass_z(d, 0, d ^ turn))
    share(gp.at[core, z])

    def z_step(hop, turn):
        for d in range(2):
            sub = d ^ turn
            pass_z(d, hop, sub).wait_recv()
            if hop < 2 or (hop == 2 and turn == 0):
                begin(pass_z(d, hop + 1, sub))
        for d in range(2):
            sign = 1 if d == 0 else -1
            if hop == 3:
                share(gp.at[core, z_at(4), pl.ds(2 * d, 2)])
            elif turn == 1:
                share(gp.at[core, z_at(-sign * (hop + 1))])

    def x_step(part_at):
        for d in range(2):
            pass_x(d, part_at).wait_recv()
            if part_at == 0:
                begin(pass_x(d, 2))
        for d in range(2):
            sign = 1 if d == 0 else -1
            half = d if part_at != 1 else 1 - d
            share(gq.at[core, x_at(-sign if part_at < 2 else 2), pl.ds(4 * half, 4)])

    z_step(0, 0)
    for copy in near_q:
        copy.wait_recv()
    for part_at in range(2):
        for d in range(2):
            begin(pass_x(d, part_at))
    share(gq.at[core, x])
    z_step(0, 1)
    z_step(1, 0)
    z_step(1, 1)
    x_step(0)
    z_step(2, 0)
    z_step(2, 1)
    x_step(1)
    z_step(3, 0)
    x_step(2)
    for copy in shared:
        copy.wait_recv()
    drain()


def communicate(partials, momentum):
    def ring(n, *block):
        return [pltpu.VMEM((2, n - 1) + block, F32)] * 2

    def sems(*shape):
        return [pltpu.SemaphoreType.DMA(shape)] * 2

    vmem = pl.BlockSpec(memory_space=pltpu.VMEM)
    block = pltpu.VMEM((ROWS, W), F32)
    return pl.pallas_call(
        kernel,
        out_shape=[
            jax.ShapeDtypeStruct((ROWS, W), F32),
            jax.ShapeDtypeStruct((4, ROWS, W), F32),
            jax.ShapeDtypeStruct((2, NZ, NX, 2, 16, 128), F32),
            jax.ShapeDtypeStruct((2, NX, NZ, 2, 24, 128), F32),
        ],
        in_specs=[pl.BlockSpec(memory_space=pl.ANY), vmem],
        out_specs=[vmem] * 4,
        scratch_shapes=[
            pltpu.VMEM((64, ROWS, W), jnp.bfloat16),
            pltpu.VMEM((2, ROWS, W), F32),
            pltpu.VMEM((2, NX, HEAD, W), F32),
            pltpu.VMEM((2, NZ, TAIL, W), F32),
            *ring(NZ, NX, HEAD, W), *ring(NX, HEAD, W),
            *ring(NX, len(FAR), TAIL, W), *ring(NX, len(MID), TAIL, W), *ring(NX, len(NEAR), TAIL, W), *ring(NZ, TAIL, W),
            block, block, block, block, block,
            pltpu.VMEM((NZ, NX, 16, 128), F32), pltpu.VMEM((NX, NZ, 24, 128), F32),
            pltpu.VMEM((NZ - 1, NX, 16, 128), F32), pltpu.VMEM((NX - 1, NZ, 24, 128), F32),
            pltpu.VMEM((NX, 16, 128), F32), pltpu.VMEM((NZ, 24, 128), F32),
            pltpu.VMEM((2 * NX, 16, 128), F32), pltpu.VMEM((2 * NZ, 24, 128), F32),
            pltpu.SemaphoreType.DMA,
            *sems(2, NZ - 1), *sems(2, NX - 1), *sems(2, NX - 1), *sems(2, NX - 1), *sems(2, NX - 1), *sems(2, NZ - 1),
            *sems(3, 2), *sems(2, 2),
            *sems(NZ - 1), *sems(NX - 1), *sems(2 * NX), *sems(2 * NZ),
            *sems(2 * NX), *sems(2 * NZ), *sems(2, 4, 2), *sems(2, 3), *sems(18),
        ],
        compiler_params=pltpu.CompilerParams(collective_id=0, has_side_effects=True, vmem_limit_bytes=52 * 1024 * 1024),
    )(partials.reshape(64, ROWS, W), momentum)


def finish(x_ref, gp, gq, w_ref, m_ref, update_ref, neww_ref, newm_ref,
           a, a2, low, ah, al, a2h, a2l, mh, ml, vh, vl, y, w):
    tp = lax.axis_index("tp")
    newm_ref[...] = m_ref[...]
    trace = jnp.zeros((1, 1), F32)
    for t in range(4):
        core, lo, base = t % 2, t // 2, 256 * t
        for xx in range(NX):
            for zz in range(NZ):
                r, c = (xx % 2) * 8 + zz, xx // 2
                a[base + 16 * r:base + 16 * r + 16, base + 128 * c:base + 128 * c + 128] = gp[core, zz, xx, lo]
                low[t, 24 * r:24 * r + 24, 128 * c:128 * c + 128] = gq[core, xx, zz, lo]
        block = a[base:base + 256, base:base + 256]
        on_diag = lax.broadcasted_iota(jnp.int32, (256, 256), 0) == lax.broadcasted_iota(jnp.int32, (256, 256), 1)
        trace = trace + jnp.sum(jnp.where(on_diag, block, 0.0), keepdims=True)
    for t in range(4):
        nxt = (t + 1) % 4
        side = low[t, :256, :]
        a[256 * nxt:256 * nxt + 256, 256 * t:256 * t + 256] = side
        a[256 * t:256 * t + 256, 256 * nxt:256 * nxt + 256] = side.T
        far = low[t, 256:, :]
        i, j = 256 * (t % 2 + 2) + 128 * (t // 2), 256 * (t % 2)
        a[i:i + 128, j:j + 256] = far
        a[j:j + 256, i:i + 128] = far.T
    inverse = 1.0 / (jnp.sqrt(trace) + NORM_EPS)
    scale = inverse * inverse

    def tiles(body):
        def step(i, carry):
            body(pl.ds(pl.multiple_of(i * 256, 256), 256), i)
            return carry
        lax.fori_loop(0, 4, step, 0)

    def prepare(rows, _):
        block = a[rows, :] * scale
        a[rows, :] = block
        ah[rows, :], al[rows, :] = split(block)

    tiles(prepare)

    def dot3(lh, ll, rh, rl):
        dot = functools.partial(jnp.dot, preferred_element_type=F32)
        return dot(lh, rh) + (dot(lh, rl) + dot(ll, rh))

    for i in range(4):
        rows = slice(256 * i, 256 * i + 256)
        for j in range(i, 4):
            cols = slice(256 * j, 256 * j + 256)
            block = dot3(ah[rows, :], al[rows, :], ah[:, cols], al[:, cols])
            a2[rows, cols] = block
            if j > i:
                a2[cols, rows] = block.T

    def mix(rows, i):
        square = a2[rows, :]
        a2h[rows, :], a2l[rows, :] = split(square)
        same = lax.broadcasted_iota(jnp.int32, (256, FF), 0) + i * 256 == lax.broadcasted_iota(jnp.int32, (256, FF), 1)
        value = COEF_B * a[rows, :] + COEF_C * square + jnp.where(same, COEF_A, 0.0)
        mh[rows, :], ml[rows, :] = split(value)

    tiles(mix)

    own = pl.ds(pl.multiple_of(tp * 256, 256), 256)

    def eye(i):
        return jnp.where(
            lax.broadcasted_iota(jnp.int32, (256, W), 0) + i * 256 == lax.broadcasted_iota(jnp.int32, (256, W), 1) + tp * 256,
            COEF_A, 0.0,
        )

    def start(rows, i):
        w[rows, :] = a[rows, own]
        value = COEF_B * a[rows, own] + COEF_C * a2[rows, own] + eye(i)
        vh[rows, :], vl[rows, :] = split(value)

    tiles(start)

    def product(high, lowp, after):
        def body(rows, i):
            y[rows, :] = after(dot3(high[rows, :], lowp[rows, :], vh[...], vl[...]), rows, i)
        tiles(body)

        def again(rows, i):
            vh[rows, :], vl[rows, :] = split(y[rows, :])
        tiles(again)

    product(mh, ml, lambda value, rows, i: value)
    product(a2h, a2l, lambda value, rows, i: COEF_B * w[rows, :] + COEF_C * value)
    product(mh, ml, lambda value, rows, i: value)
    product(mh, ml, lambda value, rows, i: value + eye(i))

    xh, xl = split(jnp.concatenate([x_ref[t] for t in range(4)], axis=1) * inverse)
    result = jnp.zeros((ROWS, W), F32)
    for t in range(4):
        cols = slice(256 * t, 256 * t + 256)
        once_h, once_l = split(dot3(xh, xl, mh[:, cols], ml[:, cols]))
        result = result + dot3(once_h, once_l, vh[cols, :], vl[cols, :])
    update = 0.2 * math.sqrt(max(D, FF)) * result
    update_ref[...] = update
    neww_ref[...] = w_ref[...] - LEARN_RATE * (update + WEIGHT_DECAY * w_ref[...])


def orthogonalize(x, gp, gq, weights, new_momentum):
    vmem = pl.BlockSpec(memory_space=pltpu.VMEM)
    block = jax.ShapeDtypeStruct((ROWS, W), F32)
    half = jnp.bfloat16
    return pl.pallas_call(
        finish,
        out_shape=[block] * 3,
        in_specs=[vmem] * 5,
        out_specs=[vmem] * 3,
        scratch_shapes=[
            pltpu.VMEM((FF, FF), F32), pltpu.VMEM((FF, FF), F32), pltpu.VMEM((4, 384, W), F32),
            *[pltpu.VMEM((FF, FF), half)] * 6,
            pltpu.VMEM((FF, W), half), pltpu.VMEM((FF, W), half),
            pltpu.VMEM((FF, W), F32), pltpu.VMEM((FF, W), F32),
        ],
        compiler_params=pltpu.CompilerParams(vmem_limit_bytes=52 * 1024 * 1024),
    )(x, gp, gq, weights, new_momentum)


def on_device(partials, momentum, weights):
    new_momentum, x, gp, gq = communicate(partials[0], momentum)
    return tuple(orthogonalize(x, gp, gq, weights, new_momentum))


def solution(mesh):
    return jax.shard_map(
        on_device,
        mesh=mesh,
        in_specs=(P("dp", None, "tp"), P("dp", "tp"), P("dp", "tp")),
        out_specs=(P("dp", "tp"), P("dp", "tp"), P("dp", "tp")),
        check_vma=False,
    )
```

time: 137 us -> 122 us (0.89)
  Pallas kernels: 134 us -> 121 us
    pallas_call x1, Pallas kernels: 112 us -> 98.1 us  [communicate(): pl.pallas_call(kernel, out_shape=[jax.ShapeDtypeStruct((ROWS, W), F32), j...]
where the time goes in v3:
time: 122 us
  Pallas kernels  121 us (99%)
    pallas_call x1, Pallas kernels, communicate(): pl.pallas_call(kernel, out_shape=[jax.ShapeDtypeStruct((ROWS, W), F32), j...  98.1 us
    pallas_call x1, Pallas kernels, orthogonalize(): pl.pallas_call(finish, out_shape=[block] * 3, in_specs=[vmem] * 5, out_sp...  22.4 us

profile of v3, /device:TPU:1, one launch (start us, length us, event | category | flops | bytes accessed | tf_op | source)
XLA Modules:
  0.0 122.1 jit_solution(5787288546427349308)
XLA Ops:
  0.6 0.0 copy-start
  0.6 0.0 copy-start.1
  0.7 0.9 copy-done.1
  1.6 98.1 %shard_map.58 = (f32[112,256]{1,0:T(8,128)S(1)}, f32[4,112,256]{2,1,0:T(8,128)S(1)}, f32[2,8,4,2,16,128]{5,4,3,2,1,0:T(8,128)S(1)}, f32[2,4,8,2,24,128]{5,4,3,2,1,0:T(8,128)}) custom-call(bf16[64,112,256]{2,1,0:T(8,128)(2,1)} %bitcast.1, f32[112,256]{1,0:T(8,128)S(1)} %copy-done.1), custom_call_target="tpu_custom_call" | custom-call | tf_op jit(solution)/shard_map/pallas_call | solution.py:417
  99.7 0.0 copy-done
  99.7 22.4 %shard_map.59 = (f32[112,256]{1,0:T(8,128)}, f32[112,256]{1,0:T(8,128)}, f32[112,256]{1,0:T(8,128)}) custom-call(f32[4,112,256]{2,1,0:T(8,128)S(1)} %get-tuple-element.7.x_ref, f32[2,8,4,2,16,128]{5,4,3,2,1,0:T(8,128)S(1)} %get-tuple-element.8.gp, f32[2,4,8,2,24,128]{5,4,3,2,1,0:T(8,128)} %get-tuple-element.9.gq, f32[112,256]{1,0:T(8,128)S(1)} %copy-done, ...), custom_call_target="tpu_custom_call" | custom-call | tf_op jit(solution)/shard_map/pallas_call | solution.py:555
Async XLA Ops:
  0.6 99.0 %copy-start = (f32[112,256]{1,0:T(8,128)S(1)}, f32[112,256]{1,0:T(8,128)}, u32[]{:S(2)}) copy-start(f32[112,256]{1,0:T(8,128)} %w_ref.1) | copy-start | bytes 344068
  0.6 0.9 copy-start.1

commit v4 on v3

--- a/solution.py
+++ b/solution.py
@@ -75,7 +75,7 @@
     return dot(lh, rh) + (dot(lh, rl) + dot(ll, rh))
 
 
-def kernel(part_hbm, mom_ref, newm_ref, xg, gp, gq, part, fin, acc_p, acc_q,
+def kernel(part_hbm, mom_hbm, newm_ref, xg, gp, gq, part, mom_ref, fin, acc_p, acc_q,
            p_send, p_recv, p2_send, p2_recv, qa_send, qa_recv, qb_send, qb_recv, qc_send, qc_recv, q2_send, q2_recv,
            same_recv, side_send, side_recv, cross_send, cross_recv,
            src_p, src_q, one_p, one_q, tot_p, tot_q, two_p, two_q,
@@ -112,8 +112,10 @@
         for copy in pending:
             copy.wait_send()
 
-    load = pltpu.make_async_copy(part_hbm, part, load_sem)
+    load = pltpu.make_async_copy(part_hbm, part, load_sem.at[0])
     load.start()
+    load_momentum = pltpu.make_async_copy(mom_hbm, mom_ref, load_sem.at[1])
+    load_momentum.start()
     peers = [at(dx, dy, 0, o) for dx in range(1, NX) for dy, o in ((0, 0), (1, 0), (0, 1))]
     peers += [at(0, dy, dz, o) for dz in range(1, NZ) for dy, o in ((0, 0), (1, 0), (0, 1))]
     peers += [at(0, 1, 0), at(0, 0, 0, 1), at(0, 1, 0, 1), sibling]
@@ -121,6 +123,7 @@
     for peer in peers:
         pl.semaphore_signal(barrier, inc=1, device_id=peer, device_id_type=MESH)
     load.wait()
+    load_momentum.wait()
     pl.semaphore_wait(barrier, len(peers))
 
     def along_z(step):
@@ -422,10 +425,11 @@
             jax.ShapeDtypeStruct((2, NZ, NX, 2, 16, 128), F32),
             jax.ShapeDtypeStruct((2, NX, NZ, 2, 24, 128), F32),
         ],
-        in_specs=[pl.BlockSpec(memory_space=pl.ANY), vmem],
+        in_specs=[pl.BlockSpec(memory_space=pltpu.HBM)] * 2,
         out_specs=[vmem] * 4,
         scratch_shapes=[
             pltpu.VMEM((64, ROWS, W), jnp.bfloat16),
+            block,
             pltpu.VMEM((2, ROWS, W), F32),
             pltpu.VMEM((2, NX, HEAD, W), F32),
             pltpu.VMEM((2, NZ, TAIL, W), F32),
@@ -436,18 +440,18 @@
             pltpu.VMEM((NZ - 1, NX, 16, 128), F32), pltpu.VMEM((NX - 1, NZ, 24, 128), F32),
             pltpu.VMEM((NX, 16, 128), F32), pltpu.VMEM((NZ, 24, 128), F32),
             pltpu.VMEM((2 * NX, 16, 128), F32), pltpu.VMEM((2 * NZ, 24, 128), F32),
-            pltpu.SemaphoreType.DMA,
+            pltpu.SemaphoreType.DMA((2,)),
             *sems(2, NZ - 1), *sems(2, NX - 1), *sems(2, NX - 1), *sems(2, NX - 1), *sems(2, NX - 1), *sems(2, NZ - 1),
             *sems(3, 2), *sems(2, 2),
             *sems(NZ - 1), *sems(NX - 1), *sems(2 * NX), *sems(2 * NZ),
             *sems(2 * NX), *sems(2 * NZ), *sems(2, 4, 2), *sems(2, 3), *sems(18),
         ],
-        compiler_params=pltpu.CompilerParams(collective_id=0, has_side_effects=True, vmem_limit_bytes=52 * 1024 * 1024),
+        compiler_params=pltpu.CompilerParams(collective_id=0, has_side_effects=True, vmem_limit_bytes=49 * 1024 * 1024),
     )(partials.reshape(64, ROWS, W), momentum)
 
 
 def finish(x_ref, gp, gq, w_ref, m_ref, update_ref, neww_ref, newm_ref,
-           a, a2, low, ah, al, a2h, a2l, mh, ml, vh, vl, y, w):
+           a, a2, low, ah, al, a2h, a2l, mh, ml, mine):
     tp = lax.axis_index("tp")
     newm_ref[...] = m_ref[...]
     trace = jnp.zeros((1, 1), F32)
@@ -508,41 +512,24 @@
 
     tiles(mix)
 
+    def times(x, high, lowp, cols=None):
+        xh, xl = split(x)
+        both = jnp.concatenate([xh, xl], axis=0)
+        parts = []
+        for at in [cols] if cols is not None else [slice(256 * j, 256 * j + 256) for j in range(4)]:
+            first = jnp.dot(both, high[:, at], preferred_element_type=F32)
+            second = jnp.dot(xh, lowp[:, at], preferred_element_type=F32)
+            parts.append(first[:ROWS] + (first[ROWS:] + second))
+        return parts[0] if cols is not None else jnp.concatenate(parts, axis=1)
+
     own = pl.ds(pl.multiple_of(tp * 256, 256), 256)
-
-    def eye(i):
-        return jnp.where(
-            lax.broadcasted_iota(jnp.int32, (256, W), 0) + i * 256 == lax.broadcasted_iota(jnp.int32, (256, W), 1) + tp * 256,
-            COEF_A, 0.0,
-        )
-
-    def start(rows, i):
-        w[rows, :] = a[rows, own]
-        value = COEF_B * a[rows, own] + COEF_C * a2[rows, own] + eye(i)
-        vh[rows, :], vl[rows, :] = split(value)
-
-    tiles(start)
-
-    def product(high, lowp, after):
-        def body(rows, i):
-            y[rows, :] = after(dot3(high[rows, :], lowp[rows, :], vh[...], vl[...]), rows, i)
-        tiles(body)
-
-        def again(rows, i):
-            vh[rows, :], vl[rows, :] = split(y[rows, :])
-        tiles(again)
-
-    product(mh, ml, lambda value, rows, i: value)
-    product(a2h, a2l, lambda value, rows, i: COEF_B * w[rows, :] + COEF_C * value)
-    product(mh, ml, lambda value, rows, i: value)
-    product(mh, ml, lambda value, rows, i: value + eye(i))
-
-    xh, xl = split(jnp.concatenate([x_ref[t] for t in range(4)], axis=1) * inverse)
-    result = jnp.zeros((ROWS, W), F32)
+    start = jnp.concatenate([x_ref[t] for t in range(4)], axis=1) * inverse
+    one = times(start, mh, ml)
     for t in range(4):
-        cols = slice(256 * t, 256 * t + 256)
-        once_h, once_l = split(dot3(xh, xl, mh[:, cols], ml[:, cols]))
-        result = result + dot3(once_h, once_l, vh[cols, :], vl[cols, :])
+        mine[t] = one[:, 256 * t:256 * t + 256]
+    turned = times(times(one, mh, ml), mh, ml)
+    result = COEF_A * mine[tp] + COEF_B * times(turned, ah, al, own)
+    result = result + COEF_C * times(times(times(turned, a2h, a2l), mh, ml), mh, ml, own)
     update = 0.2 * math.sqrt(max(D, FF)) * result
     update_ref[...] = update
     neww_ref[...] = w_ref[...] - LEARN_RATE * (update + WEIGHT_DECAY * w_ref[...])
@@ -560,10 +547,9 @@
         scratch_shapes=[
             pltpu.VMEM((FF, FF), F32), pltpu.VMEM((FF, FF), F32), pltpu.VMEM((4, 384, W), F32),
             *[pltpu.VMEM((FF, FF), half)] * 6,
-            pltpu.VMEM((FF, W), half), pltpu.VMEM((FF, W), half),
-            pltpu.VMEM((FF, W), F32), pltpu.VMEM((FF, W), F32),
+            pltpu.VMEM((4, ROWS, W), F32),
         ],
-        compiler_params=pltpu.CompilerParams(vmem_limit_bytes=52 * 1024 * 1024),
+        compiler_params=pltpu.CompilerParams(vmem_limit_bytes=40 * 1024 * 1024),
     )(x, gp, gq, weights, new_momentum)
 
 

time: 122 us -> 112 us (0.918)
  Pallas kernels: 121 us -> 110 us
    pallas_call x1, Pallas kernels: 22.4 us -> 13.2 us  [orthogonalize(): pl.pallas_call(finish, out_shape=[block] * 3, in_specs=[vmem] * 5, out_sp...]
where the time goes in v4:
time: 112 us
  Pallas kernels  110 us (98%)
    pallas_call x1, Pallas kernels, communicate(): pl.pallas_call(kernel, out_shape=[jax.ShapeDtypeStruct((ROWS, W), F32), j...  97.2 us
    pallas_call x1, Pallas kernels, orthogonalize(): pl.pallas_call(finish, out_shape=[block] * 3, in_specs=[vmem] * 5, out_sp...  13.2 us

profile of v4, /device:TPU:1, one launch (start us, length us, event | category | flops | bytes accessed | tf_op | source)
XLA Modules:
  0.0 111.9 jit_solution(14677087328048630778)
XLA Ops:
  0.6 0.0 copy-start
  0.6 0.0 copy-start.1
  0.7 0.9 copy-done.1
  1.6 97.2 %shard_map.58 = (f32[112,256]{1,0:T(8,128)S(1)}, f32[4,112,256]{2,1,0:T(8,128)S(1)}, f32[2,8,4,2,16,128]{5,4,3,2,1,0:T(8,128)S(1)}, f32[2,4,8,2,24,128]{5,4,3,2,1,0:T(8,128)S(1)}) custom-call(bf16[64,112,256]{2,1,0:T(8,128)(2,1)} %bitcast.1, f32[112,256]{1,0:T(8,128)S(1)} %copy-done.1), custom_call_target="tpu_custom_call" | custom-call | tf_op jit(solution)/shard_map/pallas_call | solution.py:420
  98.8 0.0 copy-done
  98.8 13.2 %shard_map.59 = (f32[112,256]{1,0:T(8,128)}, f32[112,256]{1,0:T(8,128)}, f32[112,256]{1,0:T(8,128)}) custom-call(f32[4,112,256]{2,1,0:T(8,128)S(1)} %get-tuple-element.7.x_ref, f32[2,8,4,2,16,128]{5,4,3,2,1,0:T(8,128)S(1)} %get-tuple-element.8.gp, f32[2,4,8,2,24,128]{5,4,3,2,1,0:T(8,128)S(1)} %get-tuple-element.9.gq, f32[112,256]{1,0:T(8,128)S(1)} %copy-done, ...), custom_call_target="tpu_custom_call" | custom-call | tf_op jit(solution)/shard_map/pallas_call | solution.py:542
Async XLA Ops:
  0.6 98.1 %copy-start = (f32[112,256]{1,0:T(8,128)S(1)}, f32[112,256]{1,0:T(8,128)}, u32[]{:S(2)}) copy-start(f32[112,256]{1,0:T(8,128)} %w_ref.1) | copy-start | bytes 344068
  0.6 0.9 copy-start.1

commit v5 on v4

--- a/solution.py
+++ b/solution.py
@@ -13,11 +13,21 @@
 NX, NY, NZ = 4, 2, 8
 ROWS = 112
 HEAD = 48
+EARLY = 16
 TAIL = ROWS - HEAD
+HEAD_RING = HEAD - EARLY
+TAIL_RING = TAIL - EARLY
+Z_ORDER = (4, 3, 5, 2, 6, 1, 7, 0)
 W = 256
-FAR = (2, 3, 4, 5, 6)
-MID = (7, 1)
-NEAR = (0,)
+X_ORDER = (2, 1, 3, 0)
+Z_ORDER = (4, 3, 5, 2, 6, 1, 7, 0)
+X_GROUPS = ((0, 1), (1, 2), (3, 1))
+Z_GROUPS = ((0, 1), (1, 2), (3, 2), (5, 2), (7, 1))
+EARLY_Z = Z_GROUPS
+UNIT = 0.026
+PRIORITY = ("y", "q4", "p1", "rp", "q0", "rqz", "rpx", "q2", "qz", "p0", "p2", "q1", "px", "rq", "q3")
+BACKLOG = 6.0
+LATE, FAR_LATE = 2.0, 3.0
 D = 7168
 FF = 1024
 COEF_A = 3.4445
@@ -30,14 +40,68 @@
 NESTEROV_GRAD = 1.0 + MOMENTUM_DECAY
 
 
+def plan(priority, backlog):
+    link, cost, needs = {}, {}, {}
+
+    def add(name, k, axis, rows, after=()):
+        link[name, k], cost[name, k], needs[name, k] = axis, rows * UNIT, set(after)
+
+    def chain(name, k):
+        return {(name, k - 2)} if k >= 2 else set()
+
+    for g, count in enumerate((1, 2, 1)):
+        for k in range(NZ - 1):
+            add("p%d" % g, k, "z", count * HEAD_RING, chain("p%d" % g, k))
+    for g, count in enumerate((1, 2, 2, 2, 1)):
+        for k in range(NX - 1):
+            add("q%d" % g, k, "x", count * TAIL_RING, chain("q%d" % g, k))
+    for k in range(NX - 1):
+        g = (k + 1) // 2
+        add("px", k, "x", HEAD_RING, chain("px", k) | {("p%d" % g, 5), ("p%d" % g, 6)})
+    for k in range(NZ - 1):
+        g = (k + 1) // 2
+        add("qz", k, "z", TAIL_RING, chain("qz", k) | {("q%d" % g, 1), ("q%d" % g, 2)})
+    if EARLY:
+        for i in range(9):
+            add("y", i, "y", EARLY * (8 if i < 4 else 4 * EARLY_Z[i - 4][1]))
+        for k in range(NZ - 1):
+            add("rp", k, "z", 2 * EARLY, chain("rp", k) | {("y", 4 + (k + 1) // 2)})
+        for k in range(NX - 1):
+            add("rq", k, "x", 4 * EARLY, chain("rq", k) | ({("y", 0)} if k == 0 else {("y", 1), ("y", 2)}))
+        add("rpx", 0, "x", 2 * EARLY, {("rp", 5), ("rp", 6), ("y", 8)})
+        add("rqz", 0, "z", 8 * EARLY, {("rq", 1), ("rq", 2), ("y", 3)})
+    free, now, flying, arrived, waiting, order = dict.fromkeys("xyz", 0.0), 0.0, [], set(), list(link), []
+    while waiting or flying:
+        for axis in "zxy":
+            while free[axis] - now < backlog:
+                ready = [t for t in waiting if link[t] == axis and needs[t] <= arrived]
+                if not ready:
+                    break
+                pick = min(ready, key=lambda t: (priority.index(t[0]), t[1]))
+                waiting.remove(pick)
+                free[axis] = max(free[axis], now) + cost[pick]
+                late = FAR_LATE if pick[0] in ("rqz", "rpx", "y") else LATE
+                flying.append((free[axis] + late, pick))
+                order.append(("issue",) + pick)
+        when, pick = min(flying)
+        flying.remove((when, pick))
+        now = max(now, when) + 0.15
+        arrived.add(pick)
+        order.append(("arrive",) + pick)
+    return order, now
+
+
 class Ring:
-    def __init__(self, n, place, send, recv, send_sem, recv_sem):
-        self.n, self.place, self.send, self.recv = n, place, send, recv
-        self.send_sem, self.recv_sem = send_sem, recv_sem
+    def __init__(self, n, place, own, send, recv, send_sem, recv_sem, span=None):
+        self.n, self.place, self.own, self.span = n, place, own, span
+        self.send, self.recv, self.send_sem, self.recv_sem = send, recv, send_sem, recv_sem
+
+    def at(self, d, k):
+        return (d, k) if self.span is None else (d, k, pl.ds(*self.span))
 
     def copy(self, d, k):
         return pltpu.make_async_remote_copy(
-            src_ref=self.send.at[d, k], dst_ref=self.recv.at[d, k],
+            src_ref=self.send.at[self.at(d, k)], dst_ref=self.recv.at[self.at(d, k)],
             send_sem=self.send_sem.at[d, k], recv_sem=self.recv_sem.at[d, k],
             device_id=self.place(1 if d == 0 else -1), device_id_type=MESH,
         )
@@ -45,17 +109,21 @@
     def offset(self, d, k):
         return (1 if d == 0 else -1) * (self.n // 2 - (k + 1) // 2)
 
-    def issue(self, k, own):
-        for d in range(2):
-            value = own(self.offset(d, k), (k + d) % 2)
+    def issue(self, k):
+        for d in range(2):
+            value = self.own(self.offset(d, k), (k + d) % 2)
             if k >= 2:
-                value = value + self.recv[d, k - 2]
-            self.send[d, k] = value
+                value = value + self.recv[self.at(d, k - 2)]
+            self.send[self.at(d, k)] = value
             self.copy(d, k).start()
 
     def arrive(self, k):
         for d in range(2):
             self.copy(d, k).wait_recv()
+
+    def total(self, half):
+        first, last = self.n - 3 + (half + 1) % 2, self.n - 3 + half
+        return self.own(0, half) + self.recv[self.at(0, first)] + self.recv[self.at(1, last)]
 
     def sent(self):
         for d in range(2):
@@ -76,10 +144,12 @@
 
 
 def kernel(part_hbm, mom_hbm, newm_ref, xg, gp, gq, part, mom_ref, fin, acc_p, acc_q,
-           p_send, p_recv, p2_send, p2_recv, qa_send, qa_recv, qb_send, qb_recv, qc_send, qc_recv, q2_send, q2_recv,
+           ry_send, ry_recv, rx_send, rx_recv, rp_send, rp_recv, rq_send, rq_recv, acc_rp, acc_rq, rp2_recv, rq2_recv,
+           p_send, p_recv, px_send, px_recv, q_send, q_recv, qz_send, qz_recv,
            same_recv, side_send, side_recv, cross_send, cross_recv,
            src_p, src_q, one_p, one_q, tot_p, tot_q, two_p, two_q,
-           load_sem, p_s, p_r, p2_s, p2_r, qa_s, qa_r, qb_s, qb_r, qc_s, qc_r, q2_s, q2_r, y_s, y_r,
+           load_sem, p_s, p_r, px_s, px_r, q_s, q_r, qz_s, qz_r, y_s, y_r,
+           early_s, early_r, rp_s, rp_r, rq_s, rq_r, rp2_s, rp2_r, rq2_s, rq2_r,
            x_s, x_r, g1p_s, g1p_r, g1q_s, g1q_r, g2p_s, g2p_r, g2q_s, g2q_r,
            ap_s, ap_r, aq_s, aq_r, az_s, az_r, ax_s, ax_r, c_s, c_r):
     dp = lax.axis_index("dp")
@@ -132,59 +202,127 @@
     def along_x(step):
         return at(step, 0, 0)
 
-    p1 = Ring(NZ, along_z, p_send, p_recv, p_s, p_r)
-    p2 = Ring(NX, along_x, p2_send, p2_recv, p2_s, p2_r)
-    qa = Ring(NX, along_x, qa_send, qa_recv, qa_s, qa_r)
-    qb = Ring(NX, along_x, qb_send, qb_recv, qb_s, qb_r)
-    qc = Ring(NX, along_x, qc_send, qc_recv, qc_s, qc_r)
-    q2 = Ring(NZ, along_z, q2_send, q2_recv, q2_s, q2_r)
-
-    def own_p1(off, half):
-        return jnp.stack([part[xx * 16 + half * 8 + z_at(off), :HEAD, :].astype(F32) for xx in range(NX)])
-
-    def own_p2(off, half):
-        return acc_p[half, x_at(off)]
-
-    def own_q(rels):
+    def early_rows(xx, yy, zz, first):
+        return part[xx * 16 + yy * 8 + zz, first:first + EARLY, :].astype(F32)
+
+    def early_copy(i):
+        if i < 4:
+            off = X_ORDER[i]
+            src, dst = rx_send.at[off], rx_recv.at[off]
+        else:
+            span = pl.ds(*EARLY_Z[i - 4])
+            src, dst = ry_send.at[span], ry_recv.at[span]
+        return remote(src, dst, early_s.at[i], early_r.at[i], at(0, 1, 0))
+
+    def early_issue(i):
+        if i < 4:
+            off = X_ORDER[i]
+            for rel in range(NZ):
+                rx_send[off, rel] = early_rows(x_at(off), 1 - yh, z_at(rel), ROWS - EARLY)
+        else:
+            first, count = EARLY_Z[i - 4]
+            for j in range(first, first + count):
+                for xx in range(NX):
+                    ry_send[j, xx] = early_rows(xx, 1 - yh, z_at(Z_ORDER[j]), HEAD_RING)
+        begin(early_copy(i))
+
+    def early_arrive(i):
+        early_copy(i).wait_recv()
+
+    def own_rp(off, half):
+        j = Z_ORDER.index(off % NZ)
+        return jnp.stack([early_rows(xx, yh, z_at(off), HEAD_RING) + ry_recv[j, xx] for xx in (2 * half, 2 * half + 1)])
+
+    def own_rq(off, half):
+        return jnp.stack([early_rows(x_at(off), yh, z_at(rel), ROWS - EARLY) + rx_recv[off % NX, rel]
+                          for rel in range(4 * half, 4 * half + 4)])
+
+    def rp2_copy(dx):
+        return remote(acc_rp.at[x_at(dx)], rp2_recv.at[dx - 1], rp2_s.at[dx - 1], rp2_r.at[dx - 1], along_x(dx))
+
+    def rq2_copy(dz):
+        return remote(acc_rq.at[dz], rq2_recv.at[dz - 1], rq2_s.at[dz - 1], rq2_r.at[dz - 1], along_z(dz))
+
+    def early_total(acc, copies, recv, rows):
+        total = acc
+        for i, copy in enumerate(copies):
+            copy.wait_recv()
+            total = total + recv[i]
+        fin[yh, rows] = total
+
+    def own_p(group):
+        first, count = X_GROUPS[group]
+
         def own(off, half):
-            return jnp.stack([part[x_at(off) * 16 + half * 8 + z_at(rel), HEAD:, :].astype(F32) for rel in rels])
+            xs = [x_at(rel) for rel in X_ORDER[first:first + count]]
+            return jnp.stack([part[xx * 16 + half * 8 + z_at(off), :HEAD_RING, :].astype(F32) for xx in xs])
         return own
 
-    own_qa, own_qb, own_qc = own_q(FAR), own_q(MID), own_q(NEAR)
-
-    def own_q2(off, half):
-        return acc_q[half, off % NZ]
-
-    def p1_final():
-        for half in range(2):
-            acc_p[half] = own_p1(0, half) + p_recv[0, 5 + (half + 1) % 2] + p_recv[1, 5 + half]
-
-    def p2_final():
-        for half in range(2):
-            fin[half, :HEAD] = own_p2(0, half) + p2_recv[0, 1 + (half + 1) % 2] + p2_recv[1, 1 + half]
-
-    def q_final(rels, own, recv):
-        for half in range(2):
-            value = own(0, half) + recv[0, 1 + (half + 1) % 2] + recv[1, 1 + half]
-            for i, rel in enumerate(rels):
-                acc_q[half, rel] = value[i]
-
-    def q2_final():
-        for half in range(2):
-            fin[half, HEAD:] = own_q2(0, half) + q2_recv[0, 5 + (half + 1) % 2] + q2_recv[1, 5 + half]
+    def own_q(group):
+        first, count = Z_GROUPS[group]
+
+        def own(off, half):
+            zs = [z_at(rel) for rel in Z_ORDER[first:first + count]]
+            return jnp.stack([part[x_at(off) * 16 + half * 8 + zz, HEAD:HEAD + TAIL_RING, :].astype(F32) for zz in zs])
+        return own
+
+    def own_px(off, half):
+        return acc_p[half, X_ORDER.index(off % NX)]
+
+    def own_qz(off, half):
+        return acc_q[half, Z_ORDER.index(off % NZ)]
+
+    rings = {
+        "px": Ring(NX, along_x, own_px, px_send, px_recv, px_s, px_r),
+        "qz": Ring(NZ, along_z, own_qz, qz_send, qz_recv, qz_s, qz_r),
+        "rp": Ring(NZ, along_z, own_rp, rp_send, rp_recv, rp_s, rp_r),
+        "rq": Ring(NX, along_x, own_rq, rq_send, rq_recv, rq_s, rq_r),
+    }
+    for g, span in enumerate(X_GROUPS):
+        rings["p%d" % g] = Ring(NZ, along_z, own_p(g), p_send, p_recv, p_s.at[g], p_r.at[g], span)
+    for g, span in enumerate(Z_GROUPS):
+        rings["q%d" % g] = Ring(NX, along_x, own_q(g), q_send, q_recv, q_s.at[g], q_r.at[g], span)
+
+    def final(name):
+        if name == "columns0":
+            early_total(acc_rp[x], [rp2_copy(dx) for dx in (1, 2, 3)], rp2_recv, pl.ds(HEAD_RING, EARLY))
+            for half in range(2):
+                fin[half, :HEAD_RING] = rings["px"].total(half)
+            columns_start(0)
+        elif name == "columns1":
+            early_total(acc_rq[0], [rq2_copy(dz) for dz in range(1, NZ)], rq2_recv, pl.ds(ROWS - EARLY, EARLY))
+            for half in range(2):
+                fin[half, HEAD:HEAD + TAIL_RING] = rings["qz"].total(half)
+            columns_start(1)
+        elif name == "rpx":
+            for half in range(2):
+                acc_rp[pl.ds(2 * half, 2)] = rings["rp"].total(half)
+            for dx in (2, 1, 3):
+                begin(rp2_copy(dx))
+        elif name == "rqz":
+            for half in range(2):
+                acc_rq[pl.ds(4 * half, 4)] = rings["rq"].total(half)
+            for dz in (4, 3, 5, 2, 6, 1, 7):
+                begin(rq2_copy(dz))
+        else:
+            acc = acc_p if name[0] == "p" else acc_q
+            for half in range(2):
+                acc[half, pl.ds(*rings[name].span)] = rings[name].total(half)
 
     def columns_start(i):
         rows = pl.ds(0, HEAD) if i == 0 else pl.ds(HEAD, TAIL)
-        begin(remote(fin.at[1 - yh, rows], same_recv.at[rows], y_s.at[0, i], y_r.at[0, i], at(0, 1, 0)))
-        cross_send[rows] = NESTEROV_GRAD * fin[1 - yh, rows]
-        begin(remote(cross_send.at[rows], cross_recv.at[rows], y_s.at[1, i], y_r.at[1, i], at(0, 1, 0, 1)))
+        half = pl.ds(0, HEAD_RING) if i == 0 else pl.ds(HEAD, TAIL_RING)
+        begin(remote(fin.at[1 - yh, half], same_recv.at[half], y_s.at[0, i], y_r.at[0, i], at(0, 1, 0)))
+        cross_send[half] = NESTEROV_GRAD * fin[1 - yh, half]
+        begin(remote(cross_send.at[half], cross_recv.at[half], y_s.at[1, i], y_r.at[1, i], at(0, 1, 0, 1)))
         side_send[rows] = NESTEROV_GRAD * fin[yh, rows] + MOMENTUM_DECAY * MOMENTUM_DECAY * mom_ref[rows]
         begin(remote(side_send.at[rows], side_recv.at[rows], y_s.at[2, i], y_r.at[2, i], at(0, 0, 0, 1)))
 
     def columns_end(i):
         rows = pl.ds(0, HEAD) if i == 0 else pl.ds(HEAD, TAIL)
-        for buf, j in ((same_recv, 0), (cross_recv, 1), (side_recv, 2)):
-            remote(buf.at[rows], buf.at[rows], y_s.at[j, i], y_r.at[j, i], sibling).wait_recv()
+        half = pl.ds(0, HEAD_RING) if i == 0 else pl.ds(HEAD, TAIL_RING)
+        for buf, j, span in ((same_recv, 0, half), (cross_recv, 1, half), (side_recv, 2, rows)):
+            remote(buf.at[span], buf.at[span], y_s.at[j, i], y_r.at[j, i], sibling).wait_recv()
         gradient = fin[yh, rows] + same_recv[rows]
         new_momentum = MOMENTUM_DECAY * mom_ref[rows] + gradient
         newm_ref[rows] = new_momentum
@@ -200,68 +338,32 @@
             other = xg.at[slot, rows]
             remote(other, other, x_s.at[j, i], x_r.at[j, i], sibling).wait_recv()
 
-    p1.issue(0, own_p1)
-    qa.issue(0, own_qa)
-    p1.issue(1, own_p1)
-    qa.issue(1, own_qa)
-    p1.arrive(0)
-    p1.issue(2, own_p1)
-    qa.arrive(0)
-    qa.issue(2, own_qa)
-    p1.arrive(1)
-    p1.issue(3, own_p1)
-    p1.arrive(2)
-    p1.issue(4, own_p1)
-    qa.arrive(1)
-    qb.issue(0, own_qb)
-    qb.issue(1, own_qb)
-    p1.arrive(3)
-    p1.issue(5, own_p1)
-    qa.arrive(2)
-    qc.issue(0, own_qc)
-    q_final(FAR, own_qa, qa_recv)
-    q2.issue(0, own_q2)
-    q2.issue(1, own_q2)
-    p1.arrive(4)
-    p1.issue(6, own_p1)
-    qb.arrive(0)
-    qb.issue(2, own_qb)
-    q2.arrive(0)
-    q2.issue(2, own_q2)
-    q2.arrive(1)
-    q2.issue(3, own_q2)
-    qb.arrive(1)
-    qc.issue(1, own_qc)
-    p1.arrive(5)
-    qb.arrive(2)
-    q_final(MID, own_qb, qb_recv)
-    qc.arrive(0)
-    qc.issue(2, own_qc)
-    p1.arrive(6)
-    p1_final()
-    p2.issue(0, own_p2)
-    p2.issue(1, own_p2)
-    q2.arrive(2)
-    q2.issue(4, own_q2)
-    q2.arrive(3)
-    q2.issue(5, own_q2)
-    q2.arrive(4)
-    q2.issue(6, own_q2)
-    p2.arrive(0)
-    p2.issue(2, own_p2)
-    qc.arrive(1)
-    qc.arrive(2)
-    q_final(NEAR, own_qc, qc_recv)
-    p2.arrive(1)
-    p2.arrive(2)
-    p2_final()
-    columns_start(0)
-    q2.arrive(5)
-    q2.arrive(6)
-    q2_final()
-    columns_start(1)
+    for rows in (pl.ds(HEAD_RING, EARLY), pl.ds(ROWS - EARLY, EARLY)):
+        same_recv[rows] = jnp.zeros((EARLY, W), F32)
+        cross_recv[rows] = jnp.zeros((EARLY, W), F32)
+    order, _ = plan(PRIORITY, BACKLOG)
+    left = {name: {(name, ring.n - 3), (name, ring.n - 2)} for name, ring in rings.items() if ring.span is not None}
+    left["columns0"] = {("px", 1), ("px", 2), ("rpx", 0), ("p2", 5), ("p2", 6)}
+    left["columns1"] = {("qz", 5), ("qz", 6), ("rqz", 0), ("q4", 1), ("q4", 2)}
+    for what, name, k in order:
+        if what == "issue":
+            if name == "y":
+                early_issue(k)
+            elif name in ("rpx", "rqz"):
+                final(name)
+            else:
+                rings[name].issue(k)
+            continue
+        if name == "y":
+            early_arrive(k)
+        elif name in rings:
+            rings[name].arrive(k)
+        for key in [key for key in left if (name, k) in left[key]]:
+            left[key].discard((name, k))
+            if not left[key]:
+                final(key)
     columns_end(0)
-    for ring in (p1, p2, qa, qb, qc, q2):
+    for ring in rings.values():
         ring.sent()
     columns_end(1)
     columns_wait(0)
@@ -431,18 +533,23 @@
             pltpu.VMEM((64, ROWS, W), jnp.bfloat16),
             block,
             pltpu.VMEM((2, ROWS, W), F32),
-            pltpu.VMEM((2, NX, HEAD, W), F32),
-            pltpu.VMEM((2, NZ, TAIL, W), F32),
-            *ring(NZ, NX, HEAD, W), *ring(NX, HEAD, W),
-            *ring(NX, len(FAR), TAIL, W), *ring(NX, len(MID), TAIL, W), *ring(NX, len(NEAR), TAIL, W), *ring(NZ, TAIL, W),
+            pltpu.VMEM((2, NX, HEAD_RING, W), F32),
+            pltpu.VMEM((2, NZ, TAIL_RING, W), F32),
+            *[pltpu.VMEM((NZ, NX, EARLY, W), F32)] * 2, *[pltpu.VMEM((NX, NZ, EARLY, W), F32)] * 2,
+            *ring(NZ, 2, EARLY, W), *ring(NX, 4, EARLY, W),
+            pltpu.VMEM((NX, EARLY, W), F32), pltpu.VMEM((NZ, EARLY, W), F32),
+            pltpu.VMEM((NX - 1, EARLY, W), F32), pltpu.VMEM((NZ - 1, EARLY, W), F32),
+            *ring(NZ, NX, HEAD_RING, W), *ring(NX, HEAD_RING, W), *ring(NX, NZ, TAIL_RING, W), *ring(NZ, TAIL_RING, W),
             block, block, block, block, block,
             pltpu.VMEM((NZ, NX, 16, 128), F32), pltpu.VMEM((NX, NZ, 24, 128), F32),
             pltpu.VMEM((NZ - 1, NX, 16, 128), F32), pltpu.VMEM((NX - 1, NZ, 24, 128), F32),
             pltpu.VMEM((NX, 16, 128), F32), pltpu.VMEM((NZ, 24, 128), F32),
             pltpu.VMEM((2 * NX, 16, 128), F32), pltpu.VMEM((2 * NZ, 24, 128), F32),
             pltpu.SemaphoreType.DMA((2,)),
-            *sems(2, NZ - 1), *sems(2, NX - 1), *sems(2, NX - 1), *sems(2, NX - 1), *sems(2, NX - 1), *sems(2, NZ - 1),
-            *sems(3, 2), *sems(2, 2),
+            *sems(3, 2, NZ - 1), *sems(2, NX - 1), *sems(5, 2, NX - 1), *sems(2, NZ - 1),
+            *sems(3, 2),
+            *sems(9), *sems(2, NZ - 1), *sems(2, NX - 1), *sems(NX - 1), *sems(NZ - 1),
+            *sems(2, 2),
             *sems(NZ - 1), *sems(NX - 1), *sems(2 * NX), *sems(2 * NZ),
             *sems(2 * NX), *sems(2 * NZ), *sems(2, 4, 2), *sems(2, 3), *sems(18),
         ],

time: 112 us -> 109 us (0.973)
  Pallas kernels: 110 us -> 107 us
    pallas_call x1, Pallas kernels: 97.2 us -> 93.9 us  [communicate(): pl.pallas_call(kernel, out_shape=[jax.ShapeDtypeStruct((ROWS, W), F32), j...]
where the time goes in v5:
time: 109 us
  Pallas kernels  107 us (98%)
    pallas_call x1, Pallas kernels, communicate(): pl.pallas_call(kernel, out_shape=[jax.ShapeDtypeStruct((ROWS, W), F32), j...  93.9 us
    pallas_call x1, Pallas kernels, orthogonalize(): pl.pallas_call(finish, out_shape=[block] * 3, in_specs=[vmem] * 5, out_sp...  13.4 us

profile of v5, /device:TPU:1, one launch (start us, length us, event | category | flops | bytes accessed | tf_op | source)
XLA Modules:
  0.0 108.8 jit_solution(5574284185553781628)
XLA Ops:
  0.6 0.0 copy-start
  0.6 0.0 copy-start.1
  0.7 0.9 copy-done.1
  1.6 93.9 %shard_map.58 = (f32[112,256]{1,0:T(8,128)S(1)}, f32[4,112,256]{2,1,0:T(8,128)S(1)}, f32[2,8,4,2,16,128]{5,4,3,2,1,0:T(8,128)S(1)}, f32[2,4,8,2,24,128]{5,4,3,2,1,0:T(8,128)S(1)}) custom-call(bf16[64,112,256]{2,1,0:T(8,128)(2,1)} %bitcast.1, f32[112,256]{1,0:T(8,128)S(1)} %copy-done.1), custom_call_target="tpu_custom_call" | custom-call | tf_op jit(solution)/shard_map/pallas_call | solution.py:522
  95.5 0.0 copy-done
  95.5 13.4 %shard_map.59 = (f32[112,256]{1,0:T(8,128)}, f32[112,256]{1,0:T(8,128)}, f32[112,256]{1,0:T(8,128)}) custom-call(f32[4,112,256]{2,1,0:T(8,128)S(1)} %get-tuple-element.7.x_ref, f32[2,8,4,2,16,128]{5,4,3,2,1,0:T(8,128)S(1)} %get-tuple-element.8.gp, f32[2,4,8,2,24,128]{5,4,3,2,1,0:T(8,128)S(1)} %get-tuple-element.9.gq, f32[112,256]{1,0:T(8,128)S(1)} %copy-done, ...), custom_call_target="tpu_custom_call" | custom-call | tf_op jit(solution)/shard_map/pallas_call | solution.py:649
Async XLA Ops:
  0.6 94.8 %copy-start = (f32[112,256]{1,0:T(8,128)S(1)}, f32[112,256]{1,0:T(8,128)}, u32[]{:S(2)}) copy-start(f32[112,256]{1,0:T(8,128)} %w_ref.1) | copy-start | bytes 344068
  0.6 0.9 copy-start.1

commit v6 on v5

--- a/solution.py
+++ b/solution.py
@@ -17,7 +17,6 @@
 TAIL = ROWS - HEAD
 HEAD_RING = HEAD - EARLY
 TAIL_RING = TAIL - EARLY
-Z_ORDER = (4, 3, 5, 2, 6, 1, 7, 0)
 W = 256
 X_ORDER = (2, 1, 3, 0)
 Z_ORDER = (4, 3, 5, 2, 6, 1, 7, 0)
@@ -392,18 +391,7 @@
     for _, copy in rq:
         begin(copy)
 
-    for _, copy in rp:
-        copy.wait_recv()
-    total = src_p[z]
-    for i in range(NZ - 1):
-        total = total + one_p[i]
-    tot_p[...] = total
     second_p, second_q = [], []
-    for dx in (2, 1, 3, 0):
-        for dy in range(2):
-            if dx or dy:
-                i = dy * NX + dx
-                second_p.append(begin(remote(tot_p.at[x_at(dx)], two_p.at[i], g2p_s.at[i], g2p_r.at[i], at(dx, dy, 0))))
     for _, copy in rq:
         copy.wait_recv()
     total = src_q[x]
@@ -415,6 +403,17 @@
             if dz or dy:
                 i = dy * NZ + dz
                 second_q.append(begin(remote(tot_q.at[z_at(dz)], two_q.at[i], g2q_s.at[i], g2q_r.at[i], at(0, dy, dz))))
+    for _, copy in rp:
+        copy.wait_recv()
+    total = src_p[z]
+    for i in range(NZ - 1):
+        total = total + one_p[i]
+    tot_p[...] = total
+    for dx in (2, 1, 3, 0):
+        for dy in range(2):
+            if dx or dy:
+                i = dy * NX + dx
+                second_p.append(begin(remote(tot_p.at[x_at(dx)], two_p.at[i], g2p_s.at[i], g2p_r.at[i], at(dx, dy, 0))))
 
     near_p, near_q = [], []
     for copy in second_p:
@@ -558,66 +557,62 @@
 
 
 def finish(x_ref, gp, gq, w_ref, m_ref, update_ref, neww_ref, newm_ref,
-           a, a2, low, ah, al, a2h, a2l, mh, ml, mine):
+           a, low, ah, al, a2h, a2l, mh, ml, mine):
     tp = lax.axis_index("tp")
     newm_ref[...] = m_ref[...]
-    trace = jnp.zeros((1, 1), F32)
+    row, col = (lax.broadcasted_iota(jnp.int32, (16, 128), axis) for axis in range(2))
+    square = jnp.zeros((16, 128), F32)
+    for t in range(4):
+        for zz in range(NZ):
+            for xx in (0, 3):
+                square = square + jnp.where(col - row == 16 * zz, gp[t % 2, zz, xx, t // 2], 0.0)
+    inverse = 1.0 / (jnp.sqrt(jnp.sum(square, keepdims=True)) + NORM_EPS)
+    scale = inverse * inverse
+
+    def put(first_row, first_col, value):
+        rows = slice(first_row, first_row + value.shape[0])
+        cols = slice(first_col, first_col + value.shape[1])
+        a[rows, cols] = value
+        ah[rows, cols], al[rows, cols] = split(value)
+
     for t in range(4):
         core, lo, base = t % 2, t // 2, 256 * t
         for xx in range(NX):
             for zz in range(NZ):
                 r, c = (xx % 2) * 8 + zz, xx // 2
-                a[base + 16 * r:base + 16 * r + 16, base + 128 * c:base + 128 * c + 128] = gp[core, zz, xx, lo]
-                low[t, 24 * r:24 * r + 24, 128 * c:128 * c + 128] = gq[core, xx, zz, lo]
-        block = a[base:base + 256, base:base + 256]
-        on_diag = lax.broadcasted_iota(jnp.int32, (256, 256), 0) == lax.broadcasted_iota(jnp.int32, (256, 256), 1)
-        trace = trace + jnp.sum(jnp.where(on_diag, block, 0.0), keepdims=True)
+                put(base + 16 * r, base + 128 * c, gp[core, zz, xx, lo] * scale)
+                low[t, 24 * r:24 * r + 24, 128 * c:128 * c + 128] = gq[core, xx, zz, lo] * scale
     for t in range(4):
         nxt = (t + 1) % 4
         side = low[t, :256, :]
-        a[256 * nxt:256 * nxt + 256, 256 * t:256 * t + 256] = side
-        a[256 * t:256 * t + 256, 256 * nxt:256 * nxt + 256] = side.T
+        put(256 * nxt, 256 * t, side)
+        put(256 * t, 256 * nxt, side.T)
         far = low[t, 256:, :]
         i, j = 256 * (t % 2 + 2) + 128 * (t // 2), 256 * (t % 2)
-        a[i:i + 128, j:j + 256] = far
-        a[j:j + 256, i:i + 128] = far.T
-    inverse = 1.0 / (jnp.sqrt(trace) + NORM_EPS)
-    scale = inverse * inverse
-
-    def tiles(body):
-        def step(i, carry):
-            body(pl.ds(pl.multiple_of(i * 256, 256), 256), i)
-            return carry
-        lax.fori_loop(0, 4, step, 0)
-
-    def prepare(rows, _):
-        block = a[rows, :] * scale
-        a[rows, :] = block
-        ah[rows, :], al[rows, :] = split(block)
-
-    tiles(prepare)
+        put(i, j, far)
+        put(j, i, far.T)
 
     def dot3(lh, ll, rh, rl):
         dot = functools.partial(jnp.dot, preferred_element_type=F32)
         return dot(lh, rh) + (dot(lh, rl) + dot(ll, rh))
+
+    same = lax.broadcasted_iota(jnp.int32, (256, 256), 0) == lax.broadcasted_iota(jnp.int32, (256, 256), 1)
+
+    def store(rows, cols, block):
+        a2h[rows, cols], a2l[rows, cols] = split(block)
+        value = COEF_B * a[rows, cols] + COEF_C * block
+        if rows == cols:
+            value = value + jnp.where(same, COEF_A, 0.0)
+        mh[rows, cols], ml[rows, cols] = split(value)
 
     for i in range(4):
         rows = slice(256 * i, 256 * i + 256)
         for j in range(i, 4):
             cols = slice(256 * j, 256 * j + 256)
             block = dot3(ah[rows, :], al[rows, :], ah[:, cols], al[:, cols])
-            a2[rows, cols] = block
+            store(rows, cols, block)
             if j > i:
-                a2[cols, rows] = block.T
-
-    def mix(rows, i):
-        square = a2[rows, :]
-        a2h[rows, :], a2l[rows, :] = split(square)
-        same = lax.broadcasted_iota(jnp.int32, (256, FF), 0) + i * 256 == lax.broadcasted_iota(jnp.int32, (256, FF), 1)
-        value = COEF_B * a[rows, :] + COEF_C * square + jnp.where(same, COEF_A, 0.0)
-        mh[rows, :], ml[rows, :] = split(value)
-
-    tiles(mix)
+                store(cols, rows, block.T)
 
     def times(x, high, lowp, cols=None):
         xh, xl = split(x)
@@ -652,7 +647,7 @@
         in_specs=[vmem] * 5,
         out_specs=[vmem] * 3,
         scratch_shapes=[
-            pltpu.VMEM((FF, FF), F32), pltpu.VMEM((FF, FF), F32), pltpu.VMEM((4, 384, W), F32),
+            pltpu.VMEM((FF, FF), F32), pltpu.VMEM((4, 384, W), F32),
             *[pltpu.VMEM((FF, FF), half)] * 6,
             pltpu.VMEM((4, ROWS, W), F32),
         ],

time: 109 us -> 106 us (0.972)
  Pallas kernels: 107 us -> 104 us
    pallas_call x1, Pallas kernels: 13.4 us -> 10.4 us  [orthogonalize(): pl.pallas_call(finish, out_shape=[block] * 3, in_specs=[vmem] * 5, out_sp...]
where the time goes in v6:
time: 106 us; the launch traced here: 105 us
  Pallas kernels  104 us (98%)
    pallas_call x1, Pallas kernels, communicate(): pl.pallas_call(kernel, out_shape=[jax.ShapeDtypeStruct((ROWS, W), F32), j...  93.5 us
    pallas_call x1, Pallas kernels, orthogonalize(): pl.pallas_call(finish, out_shape=[block] * 3, in_specs=[vmem] * 5, out_sp...  10.4 us

profile of v6, /device:TPU:1, one launch (start us, length us, event | category | flops | bytes accessed | tf_op | source)
XLA Modules:
  0.0 105.4 jit_solution(4780084083871497922)
XLA Ops:
  0.6 0.0 copy-start
  0.6 0.0 copy-start.1
  0.7 0.9 copy-done.1
  1.6 93.5 %shard_map.58 = (f32[112,256]{1,0:T(8,128)S(1)}, f32[4,112,256]{2,1,0:T(8,128)S(1)}, f32[2,8,4,2,16,128]{5,4,3,2,1,0:T(8,128)S(1)}, f32[2,4,8,2,24,128]{5,4,3,2,1,0:T(8,128)S(1)}) custom-call(bf16[64,112,256]{2,1,0:T(8,128)(2,1)} %bitcast.1, f32[112,256]{1,0:T(8,128)S(1)} %copy-done.1), custom_call_target="tpu_custom_call" | custom-call | tf_op jit(solution)/shard_map/pallas_call | solution.py:521
  95.0 0.0 copy-done
  95.1 10.4 %shard_map.59 = (f32[112,256]{1,0:T(8,128)}, f32[112,256]{1,0:T(8,128)}, f32[112,256]{1,0:T(8,128)}) custom-call(f32[4,112,256]{2,1,0:T(8,128)S(1)} %get-tuple-element.7.x_ref, f32[2,8,4,2,16,128]{5,4,3,2,1,0:T(8,128)S(1)} %get-tuple-element.8.gp, f32[2,4,8,2,24,128]{5,4,3,2,1,0:T(8,128)S(1)} %get-tuple-element.9.gq, f32[112,256]{1,0:T(8,128)S(1)} %copy-done, ...), custom_call_target="tpu_custom_call" | custom-call | tf_op jit(solution)/shard_map/pallas_call | solution.py:644
Async XLA Ops:
  0.6 94.4 %copy-start = (f32[112,256]{1,0:T(8,128)S(1)}, f32[112,256]{1,0:T(8,128)}, u32[]{:S(2)}) copy-start(f32[112,256]{1,0:T(8,128)} %w_ref.1) | copy-start | bytes 344068
  0.6 0.9 copy-start.1

commit v7 on v6

--- a/solution.py
+++ b/solution.py
@@ -181,25 +181,23 @@
         for copy in pending:
             copy.wait_send()
 
+    def along_z(step):
+        return at(0, 0, step)
+
+    def along_x(step):
+        return at(step, 0, 0)
+
     load = pltpu.make_async_copy(part_hbm, part, load_sem.at[0])
     load.start()
     load_momentum = pltpu.make_async_copy(mom_hbm, mom_ref, load_sem.at[1])
     load_momentum.start()
-    peers = [at(dx, dy, 0, o) for dx in range(1, NX) for dy, o in ((0, 0), (1, 0), (0, 1))]
-    peers += [at(0, dy, dz, o) for dz in range(1, NZ) for dy, o in ((0, 0), (1, 0), (0, 1))]
-    peers += [at(0, 1, 0), at(0, 0, 0, 1), at(0, 1, 0, 1), sibling]
+    peers = [along_z(1), along_z(-1), along_x(1), along_x(-1), at(0, 1, 0), at(0, 0, 0, 1), at(0, 1, 0, 1), sibling]
     barrier = pltpu.get_barrier_semaphore()
     for peer in peers:
         pl.semaphore_signal(barrier, inc=1, device_id=peer, device_id_type=MESH)
     load.wait()
     load_momentum.wait()
     pl.semaphore_wait(barrier, len(peers))
-
-    def along_z(step):
-        return at(0, 0, step)
-
-    def along_x(step):
-        return at(step, 0, 0)
 
     def early_rows(xx, yy, zz, first):
         return part[xx * 16 + yy * 8 + zz, first:first + EARLY, :].astype(F32)

time: 106 us -> 104 us (0.981)
  Pallas kernels: 104 us -> 102 us
    pallas_call x1, Pallas kernels: 93.5 us -> 91.6 us  [communicate(): pl.pallas_call(kernel, out_shape=[jax.ShapeDtypeStruct((ROWS, W), F32), j...]
where the time goes in v7:
time: 104 us
  Pallas kernels  102 us (98%)
    pallas_call x1, Pallas kernels, communicate(): pl.pallas_call(kernel, out_shape=[jax.ShapeDtypeStruct((ROWS, W), F32), j...  91.6 us
    pallas_call x1, Pallas kernels, orthogonalize(): pl.pallas_call(finish, out_shape=[block] * 3, in_specs=[vmem] * 5, out_sp...  10.4 us

profile of v7, /device:TPU:1, one launch (start us, length us, event | category | flops | bytes accessed | tf_op | source)
XLA Modules:
  0.0 103.5 jit_solution(12715277511223691612)
XLA Ops:
  0.6 0.0 copy-start
  0.6 0.0 copy-start.1
  0.7 0.9 copy-done.1
  1.6 91.6 %shard_map.58 = (f32[112,256]{1,0:T(8,128)S(1)}, f32[4,112,256]{2,1,0:T(8,128)S(1)}, f32[2,8,4,2,16,128]{5,4,3,2,1,0:T(8,128)S(1)}, f32[2,4,8,2,24,128]{5,4,3,2,1,0:T(8,128)S(1)}) custom-call(bf16[64,112,256]{2,1,0:T(8,128)(2,1)} %bitcast.1, f32[112,256]{1,0:T(8,128)S(1)} %copy-done.1), custom_call_target="tpu_custom_call" | custom-call | tf_op jit(solution)/shard_map/pallas_call | solution.py:519
  93.1 0.0 copy-done
  93.2 10.4 %shard_map.59 = (f32[112,256]{1,0:T(8,128)}, f32[112,256]{1,0:T(8,128)}, f32[112,256]{1,0:T(8,128)}) custom-call(f32[4,112,256]{2,1,0:T(8,128)S(1)} %get-tuple-element.7.x_ref, f32[2,8,4,2,16,128]{5,4,3,2,1,0:T(8,128)S(1)} %get-tuple-element.8.gp, f32[2,4,8,2,24,128]{5,4,3,2,1,0:T(8,128)S(1)} %get-tuple-element.9.gq, f32[112,256]{1,0:T(8,128)S(1)} %copy-done, ...), custom_call_target="tpu_custom_call" | custom-call | tf_op jit(solution)/shard_map/pallas_call | solution.py:642
Async XLA Ops:
  0.6 92.5 %copy-start = (f32[112,256]{1,0:T(8,128)S(1)}, f32[112,256]{1,0:T(8,128)}, u32[]{:S(2)}) copy-start(f32[112,256]{1,0:T(8,128)} %w_ref.1) | copy-start | bytes 344068
  0.6 0.9 copy-start.1

commit v8 on v7

--- a/solution.py
+++ b/solution.py
@@ -24,8 +24,8 @@
 Z_GROUPS = ((0, 1), (1, 2), (3, 2), (5, 2), (7, 1))
 EARLY_Z = Z_GROUPS
 UNIT = 0.026
-PRIORITY = ("y", "q4", "p1", "rp", "q0", "rqz", "rpx", "q2", "qz", "p0", "p2", "q1", "px", "rq", "q3")
-BACKLOG = 6.0
+PRIORITY = ("q0", "rp", "q2", "rqz", "rpx", "px", "p1", "q4", "p2", "p0", "q1", "qz", "rq", "q3", "y")
+BACKLOG = 5.0
 LATE, FAR_LATE = 2.0, 3.0
 D = 7168
 FF = 1024
@@ -177,9 +177,9 @@
         pending.append(copy)
         return copy
 
-    def drain():
-        for copy in pending:
-            copy.wait_send()
+    def drain(keep=0):
+        while len(pending) > keep:
+            pending.pop(0).wait_send()
 
     def along_z(step):
         return at(0, 0, step)
@@ -187,16 +187,23 @@
     def along_x(step):
         return at(step, 0, 0)
 
-    load = pltpu.make_async_copy(part_hbm, part, load_sem.at[0])
-    load.start()
-    load_momentum = pltpu.make_async_copy(mom_hbm, mom_ref, load_sem.at[1])
-    load_momentum.start()
+    loads = {}
+    for rel in X_ORDER:
+        rows = pl.ds(x_at(rel) * 16, 16)
+        loads[rel] = pltpu.make_async_copy(part_hbm.at[rows], part.at[rows], load_sem.at[rel])
+        loads[rel].start()
+    loads["momentum"] = pltpu.make_async_copy(mom_hbm, mom_ref, load_sem.at[NX])
+    loads["momentum"].start()
+
+    def need(*names):
+        for name in names:
+            if name in loads:
+                loads.pop(name).wait()
+
     peers = [along_z(1), along_z(-1), along_x(1), along_x(-1), at(0, 1, 0), at(0, 0, 0, 1), at(0, 1, 0, 1), sibling]
     barrier = pltpu.get_barrier_semaphore()
     for peer in peers:
         pl.semaphore_signal(barrier, inc=1, device_id=peer, device_id_type=MESH)
-    load.wait()
-    load_momentum.wait()
     pl.semaphore_wait(barrier, len(peers))
 
     def early_rows(xx, yy, zz, first):
@@ -214,9 +221,11 @@
     def early_issue(i):
         if i < 4:
             off = X_ORDER[i]
+            need(off)
             for rel in range(NZ):
                 rx_send[off, rel] = early_rows(x_at(off), 1 - yh, z_at(rel), ROWS - EARLY)
         else:
+            need(*X_ORDER)
             first, count = EARLY_Z[i - 4]
             for j in range(first, first + count):
                 for xx in range(NX):
@@ -227,10 +236,12 @@
         early_copy(i).wait_recv()
 
     def own_rp(off, half):
+        need(*X_ORDER)
         j = Z_ORDER.index(off % NZ)
         return jnp.stack([early_rows(xx, yh, z_at(off), HEAD_RING) + ry_recv[j, xx] for xx in (2 * half, 2 * half + 1)])
 
     def own_rq(off, half):
+        need(off % NX)
         return jnp.stack([early_rows(x_at(off), yh, z_at(rel), ROWS - EARLY) + rx_recv[off % NX, rel]
                           for rel in range(4 * half, 4 * half + 4)])
 
@@ -251,6 +262,7 @@
         first, count = X_GROUPS[group]
 
         def own(off, half):
+            need(*X_ORDER[first:first + count])
             xs = [x_at(rel) for rel in X_ORDER[first:first + count]]
             return jnp.stack([part[xx * 16 + half * 8 + z_at(off), :HEAD_RING, :].astype(F32) for xx in xs])
         return own
@@ -259,6 +271,7 @@
         first, count = Z_GROUPS[group]
 
         def own(off, half):
+            need(off % NX)
             zs = [z_at(rel) for rel in Z_ORDER[first:first + count]]
             return jnp.stack([part[x_at(off) * 16 + half * 8 + zz, HEAD:HEAD + TAIL_RING, :].astype(F32) for zz in zs])
         return own
@@ -307,6 +320,7 @@
                 acc[half, pl.ds(*rings[name].span)] = rings[name].total(half)
 
     def columns_start(i):
+        need("momentum")
         rows = pl.ds(0, HEAD) if i == 0 else pl.ds(HEAD, TAIL)
         half = pl.ds(0, HEAD_RING) if i == 0 else pl.ds(HEAD, TAIL_RING)
         begin(remote(fin.at[1 - yh, half], same_recv.at[half], y_s.at[0, i], y_r.at[0, i], at(0, 1, 0)))
@@ -360,8 +374,6 @@
             if not left[key]:
                 final(key)
     columns_end(0)
-    for ring in rings.values():
-        ring.sent()
     columns_end(1)
     columns_wait(0)
 
@@ -388,6 +400,8 @@
           for dx in (2, 1, 3)]
     for _, copy in rq:
         begin(copy)
+    for ring in rings.values():
+        ring.sent()
 
     second_p, second_q = [], []
     for _, copy in rq:
@@ -439,6 +453,8 @@
                 i = dy * NZ + dz
                 near_q.append(begin(remote(mine_q, mine_q, aq_s.at[i], aq_r.at[i], at(0, 0, dz, dy))))
 
+    drain(len(near_p) + len(near_q))
+
     def pass_z(d, hop, sub):
         sign = 1 if d == 0 else -1
         chunk = gp.at[core, z_at(-sign * hop), pl.ds(2 * sub, 2)]
@@ -454,7 +470,8 @@
 
     def share(chunk):
         i = len(shared)
-        shared.append(begin(remote(chunk, chunk, c_s.at[i], c_r.at[i], sibling)))
+        shared.append(remote(chunk, chunk, c_s.at[i], c_r.at[i], sibling))
+        shared[-1].start()
 
     for copy in near_p:
         copy.wait_recv()
@@ -502,9 +519,9 @@
     x_step(1)
     z_step(3, 0)
     x_step(2)
+    drain()
     for copy in shared:
-        copy.wait_recv()
-    drain()
+        copy.wait()
 
 
 def communicate(partials, momentum):
@@ -542,7 +559,7 @@
             pltpu.VMEM((NZ - 1, NX, 16, 128), F32), pltpu.VMEM((NX - 1, NZ, 24, 128), F32),
             pltpu.VMEM((NX, 16, 128), F32), pltpu.VMEM((NZ, 24, 128), F32),
             pltpu.VMEM((2 * NX, 16, 128), F32), pltpu.VMEM((2 * NZ, 24, 128), F32),
-            pltpu.SemaphoreType.DMA((2,)),
+            pltpu.SemaphoreType.DMA((NX + 1,)),
             *sems(3, 2, NZ - 1), *sems(2, NX - 1), *sems(5, 2, NX - 1), *sems(2, NZ - 1),
             *sems(3, 2),
             *sems(9), *sems(2, NZ - 1), *sems(2, NX - 1), *sems(NX - 1), *sems(NZ - 1),

time: 104 us -> 103 us (level)
  no operation moved by 1% of the time
where the time goes in v8:
time: 103 us
  Pallas kernels  101 us (98%)
    pallas_call x1, Pallas kernels, communicate(): pl.pallas_call(kernel, out_shape=[jax.ShapeDtypeStruct((ROWS, W), F32), j...  91 us
    pallas_call x1, Pallas kernels, orthogonalize(): pl.pallas_call(finish, out_shape=[block] * 3, in_specs=[vmem] * 5, out_sp...  10.4 us

profile of v8, /device:TPU:1, one launch (start us, length us, event | category | flops | bytes accessed | tf_op | source)
XLA Modules:
  0.0 103.0 jit_solution(7457303005889883968)
XLA Ops:
  0.6 0.0 copy-start
  0.6 0.0 copy-start.1
  0.7 0.9 copy-done.1
  1.6 91.0 %shard_map.58 = (f32[112,256]{1,0:T(8,128)S(1)}, f32[4,112,256]{2,1,0:T(8,128)S(1)}, f32[2,8,4,2,16,128]{5,4,3,2,1,0:T(8,128)S(1)}, f32[2,4,8,2,24,128]{5,4,3,2,1,0:T(8,128)S(1)}) custom-call(bf16[64,112,256]{2,1,0:T(8,128)(2,1)} %bitcast.1, f32[112,256]{1,0:T(8,128)S(1)} %copy-done.1), custom_call_target="tpu_custom_call" | custom-call | tf_op jit(solution)/shard_map/pallas_call | solution.py:536
  92.6 0.0 copy-done
  92.6 10.4 %shard_map.59 = (f32[112,256]{1,0:T(8,128)}, f32[112,256]{1,0:T(8,128)}, f32[112,256]{1,0:T(8,128)}) custom-call(f32[4,112,256]{2,1,0:T(8,128)S(1)} %get-tuple-element.7.x_ref, f32[2,8,4,2,16,128]{5,4,3,2,1,0:T(8,128)S(1)} %get-tuple-element.8.gp, f32[2,4,8,2,24,128]{5,4,3,2,1,0:T(8,128)S(1)} %get-tuple-element.9.gq, f32[112,256]{1,0:T(8,128)S(1)} %copy-done, ...), custom_call_target="tpu_custom_call" | custom-call | tf_op jit(solution)/shard_map/pallas_call | solution.py:659
Async XLA Ops:
  0.6 91.9 %copy-start = (f32[112,256]{1,0:T(8,128)S(1)}, f32[112,256]{1,0:T(8,128)}, u32[]{:S(2)}) copy-start(f32[112,256]{1,0:T(8,128)} %w_ref.1) | copy-start | bytes 344068
  0.6 0.9 copy-start.1

commit v9 on v8

--- a/solution.py
+++ b/solution.py
@@ -512,11 +512,11 @@
     share(gq.at[core, x])
     z_step(0, 1)
     z_step(1, 0)
+    x_step(0)
     z_step(1, 1)
-    x_step(0)
     z_step(2, 0)
+    x_step(1)
     z_step(2, 1)
-    x_step(1)
     z_step(3, 0)
     x_step(2)
     drain()

time: 103 us -> 103 us (level)
  no operation moved by 1% of the time
where the time goes in v9:
time: 103 us
  Pallas kernels  102 us (99%)
    pallas_call x1, Pallas kernels, communicate(): pl.pallas_call(kernel, out_shape=[jax.ShapeDtypeStruct((ROWS, W), F32), j...  91.1 us
    pallas_call x1, Pallas kernels, orthogonalize(): pl.pallas_call(finish, out_shape=[block] * 3, in_specs=[vmem] * 5, out_sp...  10.4 us

profile of v9, /device:TPU:1, one launch (start us, length us, event | category | flops | bytes accessed | tf_op | source)
XLA Modules:
  0.0 103.1 jit_solution(15753300310570565404)
XLA Ops:
  0.6 0.0 copy-start
  0.6 0.0 copy-start.1
  0.7 0.9 copy-done.1
  1.6 91.1 %shard_map.58 = (f32[112,256]{1,0:T(8,128)S(1)}, f32[4,112,256]{2,1,0:T(8,128)S(1)}, f32[2,8,4,2,16,128]{5,4,3,2,1,0:T(8,128)S(1)}, f32[2,4,8,2,24,128]{5,4,3,2,1,0:T(8,128)S(1)}) custom-call(bf16[64,112,256]{2,1,0:T(8,128)(2,1)} %bitcast.1, f32[112,256]{1,0:T(8,128)S(1)} %copy-done.1), custom_call_target="tpu_custom_call" | custom-call | tf_op jit(solution)/shard_map/pallas_call | solution.py:536
  92.7 0.0 copy-done
  92.7 10.4 %shard_map.59 = (f32[112,256]{1,0:T(8,128)}, f32[112,256]{1,0:T(8,128)}, f32[112,256]{1,0:T(8,128)}) custom-call(f32[4,112,256]{2,1,0:T(8,128)S(1)} %get-tuple-element.7.x_ref, f32[2,8,4,2,16,128]{5,4,3,2,1,0:T(8,128)S(1)} %get-tuple-element.8.gp, f32[2,4,8,2,24,128]{5,4,3,2,1,0:T(8,128)S(1)} %get-tuple-element.9.gq, f32[112,256]{1,0:T(8,128)S(1)} %copy-done, ...), custom_call_target="tpu_custom_call" | custom-call | tf_op jit(solution)/shard_map/pallas_call | solution.py:659
Async XLA Ops:
  0.6 92.1 %copy-start = (f32[112,256]{1,0:T(8,128)S(1)}, f32[112,256]{1,0:T(8,128)}, u32[]{:S(2)}) copy-start(f32[112,256]{1,0:T(8,128)} %w_ref.1) | copy-start | bytes 344068
  0.6 0.9 copy-start.1
